TPU v7x, 32 devices: a whole 2x2x4 slice. The times are simulated.
32 devices in a mesh: dp: 8 (over z, y), ctx: 4 (over x, core).
Axes of the slice: x: 2, y: 2, z: 4, core: 2. Of those that a mesh axis runs over, the one named last changes fastest.
Arguments:
- tokens: bfloat16 [2, 2048, 896], P(None, ('dp', 'ctx')), may hold values from -6 to 6
- seq_lengths: int32 [8, 2, 3], P('dp'), may hold values from 1 to 254, as said below
- attn_params: bfloat16 [1839104], P(('dp', 'ctx'))
- ffn_weight: bfloat16 [3, 4864, 896], P(None, ('dp', 'ctx'))
- out_grad: bfloat16 [2, 2048, 896], P(None, ('dp', 'ctx')), may hold values from -6 to 6
Outputs:
- output: bfloat16 [2, 2048, 896], P(None, ('dp', 'ctx'))
- input_grad: bfloat16 [2, 2048, 896], P(None, ('dp', 'ctx'))
- attn_grad: float32 [1839104], P(('dp', 'ctx'))
- ffn_grad: float32 [3, 4864, 896], P(None, ('dp', 'ctx'))
Inputs may be any that keep to these rules, and one draw needn't show every extreme that they name: seq_lengths[g, m, :] are the lengths of 3 sequences packed in order from slot 0 of stream g of micro-batch m; their sum is at most 256, the other slots are padding.
All inputs are finite; a program needn't handle non-finite values.
Results may differ from a plain program's by a relative error of at most 0.013.
Values may be sent and summed in bfloat16 or wider, within the bound.
A program may use at most 256 MiB of HBM per device.

v0:
```python
import math

import jax
import jax.numpy as jnp
from jax import lax
from jax.sharding import PartitionSpec as P

D = 896
HEADS = 14
KV_HEADS = 2
HEAD = 64


EPSILON = 1e-06
THETA = 1000000.0


def rms_norm(values, gain_vec):
    return (
        values * lax.rsqrt(jnp.mean(values * values, axis=-1, keepdims=True) + EPSILON) * gain_vec
    )


def rotate(values, cosine, sine_table):
    half_width = values.shape[-1] // 2
    turned = jnp.concatenate([-values[..., half_width:], values[..., :half_width]], axis=-1)
    return values * cosine + turned * sine_table


def rotate_back(incoming, cosine, sine_table):
    scaled = incoming * sine_table
    half_width = incoming.shape[-1] // 2
    turned = jnp.concatenate([scaled[..., half_width:], -scaled[..., :half_width]], axis=-1)
    return incoming * cosine + turned


def gated_unit(gate_out, up_out):
    return jax.nn.silu(gate_out) * up_out


def geometry(seq_lens, slot_ids):
    seq_ends = jnp.cumsum(seq_lens)
    seq_starts = seq_ends - seq_lens
    filled = seq_ends[-1]
    numbers = jnp.arange(seq_lens.shape[0], dtype=jnp.int32)
    segment = jnp.sum((slot_ids[:, None] >= seq_ends[None, :]).astype(jnp.int32), axis=1)
    seq_begin = jnp.sum(
        jnp.where(segment[:, None] == numbers[None, :], seq_starts[None, :], 0), axis=1
    )
    inside = slot_ids < filled
    segment = jnp.where(inside, segment, seq_lens.shape[0] + slot_ids)
    position = jnp.where(inside, slot_ids - seq_begin, 0)
    return (segment, position)


def rotary_tables(position):
    half_width = HEAD // 2
    frequency = jnp.power(THETA, -(jnp.arange(half_width, dtype=jnp.float32) * 2.0 / HEAD))
    angles = position.astype(jnp.float32)[:, None] * frequency[None, :]
    cosine = jnp.concatenate([jnp.cos(angles), jnp.cos(angles)], axis=-1)
    sine_table = jnp.concatenate([jnp.sin(angles), jnp.sin(angles)], axis=-1)
    return (cosine, sine_table)


def unpack(flat_params):
    kv_width = KV_HEADS * HEAD
    shapes_list = [
        (D, D),
        (D, kv_width),
        (D, kv_width),
        (D, D),
        (D,),
        (kv_width,),
        (kv_width,),
        (D,),
        (D,),
    ]
    pieces = []
    offset = 0
    for piece_shape in shapes_list:
        entries = math.prod(piece_shape)
        pieces.append(flat_params[offset : offset + entries].reshape(piece_shape))
        offset += entries
    return pieces


def pack_grads(pieces, total_length):
    flat_grad = jnp.concatenate([piece.reshape(-1) for piece in pieces])
    padding = total_length - flat_grad.shape[0]
    return jnp.concatenate([flat_grad, jnp.zeros((padding,), jnp.float32)])


def ffn_fold(columns, pieces):
    normed_rows, cot_rows = pieces
    grad_gate = jnp.einsum("tf,td->fd", columns[0], normed_rows, preferred_element_type=jnp.float32)
    grad_up = jnp.einsum("tf,td->fd", columns[1], normed_rows, preferred_element_type=jnp.float32)
    grad_down = jnp.einsum("tf,td->fd", columns[2], cot_rows, preferred_element_type=jnp.float32)
    return jnp.stack([grad_gate, grad_up, grad_down], axis=0)


def per_device(tokens, seq_lengths, attn_params, ffn_weight, out_grad):
    micro_count = tokens.shape[0]
    rows_own = tokens.shape[1]
    stream = rows_own * lax.axis_size("ctx")
    group_size = HEADS // KV_HEADS
    kv_width = KV_HEADS * HEAD
    score_scale = HEAD ** (-0.5)
    slot_ids = jnp.arange(stream, dtype=jnp.int32)
    first_slot = lax.axis_index("ctx") * rows_own
    own_slots = first_slot + jnp.arange(rows_own, dtype=jnp.int32)
    total_length = attn_params.shape[0] * lax.axis_size(("dp", "ctx"))
    grad_pieces = None
    outputs = []
    input_grads = []
    kept_normed = []
    kept_gate = []
    kept_up = []
    kept_hidden = []
    kept_cot = []
    for micro in range(micro_count):
        attn_all, ffn_all = (
            lax.all_gather(attn_params, ("dp", "ctx"), axis=0, tiled=True),
            lax.all_gather(ffn_weight, ("dp", "ctx"), axis=1, tiled=True),
        )
        w_query, w_key, w_value, w_out, b_query, b_key, b_value, gain_one, gain_two = unpack(
            attn_all
        )
        w_gate = ffn_all[0]
        w_up = ffn_all[1]
        w_down = ffn_all[2]
        segment, position = geometry(seq_lengths[0, micro], slot_ids)
        own_segment = lax.dynamic_slice_in_dim(segment, first_slot, rows_own)
        own_position = lax.dynamic_slice_in_dim(position, first_slot, rows_own)
        cosine, sine_table = rotary_tables(own_position)
        cos_heads = cosine[:, None, :]
        sin_heads = sine_table[:, None, :]
        allowed = (own_segment[:, None] == segment[None, :]) & (
            slot_ids[None, :] <= own_slots[:, None]
        )
        x_float = tokens[micro].astype(jnp.float32)
        normed, norm_pull = jax.vjp(rms_norm, x_float, gain_one.astype(jnp.float32))
        normed_low = normed.astype(jnp.bfloat16)
        query_pre = jnp.dot(
            normed_low, w_query, preferred_element_type=jnp.float32
        ) + b_query.astype(jnp.float32)
        key_pre = jnp.dot(normed_low, w_key, preferred_element_type=jnp.float32) + b_key.astype(
            jnp.float32
        )
        value_pre = jnp.dot(
            normed_low, w_value, preferred_element_type=jnp.float32
        ) + b_value.astype(jnp.float32)
        query_low = rotate(query_pre.reshape(rows_own, HEADS, HEAD), cos_heads, sin_heads).astype(
            jnp.bfloat16
        )
        query_low = query_low.reshape(rows_own, KV_HEADS, group_size, HEAD)
        key_low = rotate(key_pre.reshape(rows_own, KV_HEADS, HEAD), cos_heads, sin_heads).astype(
            jnp.bfloat16
        )
        value_low = value_pre.astype(jnp.bfloat16)
        keys_all, values_all = (
            lax.all_gather(key_low.reshape(rows_own, kv_width), "ctx", axis=0, tiled=True),
            lax.all_gather(value_low, "ctx", axis=0, tiled=True),
        )
        keys_all = keys_all.reshape(stream, KV_HEADS, HEAD)
        values_all = values_all.reshape(stream, KV_HEADS, HEAD)
        scores = (
            jnp.einsum("qkgd,skd->kgqs", query_low, keys_all, preferred_element_type=jnp.float32)
            * score_scale
        )
        scores = jnp.where(allowed[None, None], scores, -1e30)
        row_max = jnp.max(scores, axis=-1, keepdims=True)
        log_total = row_max + jnp.log(jnp.sum(jnp.exp(scores - row_max), axis=-1, keepdims=True))
        soft_probs = jnp.exp(scores - log_total)
        probs_low = soft_probs.astype(jnp.bfloat16)
        mixed = jnp.einsum(
            "kgqs,skd->qkgd", probs_low, values_all, preferred_element_type=jnp.float32
        )
        mixed_low = mixed.reshape(rows_own, HEADS * HEAD).astype(jnp.bfloat16)
        second = x_float + jnp.dot(mixed_low, w_out, preferred_element_type=jnp.float32)
        normed_two, norm_two_pull = jax.vjp(rms_norm, second, gain_two.astype(jnp.float32))
        two_low = normed_two.astype(jnp.bfloat16)
        gate_out = jnp.einsum("td,fd->tf", two_low, w_gate, preferred_element_type=jnp.float32)
        up_out = jnp.einsum("td,fd->tf", two_low, w_up, preferred_element_type=jnp.float32)
        activated, unit_pull = jax.vjp(gated_unit, gate_out, up_out)
        hidden_low = activated.astype(jnp.bfloat16)
        result = second + jnp.einsum(
            "tf,fd->td", hidden_low, w_down, preferred_element_type=jnp.float32
        )
        outputs.append(result.astype(jnp.bfloat16))
        cot_low = out_grad[micro]
        d_hidden = jnp.einsum("td,fd->tf", cot_low, w_down, preferred_element_type=jnp.float32)
        d_gate, d_up = unit_pull(d_hidden)
        gate_low = d_gate.astype(jnp.bfloat16)
        up_low = d_up.astype(jnp.bfloat16)
        d_two = jnp.einsum("tf,fd->td", gate_low, w_gate, preferred_element_type=jnp.float32)
        d_two = d_two + jnp.einsum("tf,fd->td", up_low, w_up, preferred_element_type=jnp.float32)
        d_second_part, d_gain_two = norm_two_pull(d_two)
        d_second = cot_low.astype(jnp.float32) + d_second_part
        branch_low = d_second.astype(jnp.bfloat16)
        d_mixed = jnp.einsum("te,de->td", branch_low, w_out, preferred_element_type=jnp.float32)
        dmix_low = d_mixed.astype(jnp.bfloat16).reshape(rows_own, KV_HEADS, group_size, HEAD)
        again = (
            jnp.einsum("qkgd,skd->kgqs", query_low, keys_all, preferred_element_type=jnp.float32)
            * score_scale
        )
        again = jnp.where(allowed[None, None], again, -1e30)
        soft_again = jnp.exp(again - log_total)
        d_probs = jnp.einsum(
            "qkgd,skd->kgqs", dmix_low, values_all, preferred_element_type=jnp.float32
        )
        row_delta = jnp.sum(soft_again * d_probs, axis=-1, keepdims=True)
        dscore_low = (soft_again * (d_probs - row_delta)).astype(jnp.bfloat16)
        dq_rot = (
            jnp.einsum("kgqs,skd->qkgd", dscore_low, keys_all, preferred_element_type=jnp.float32)
            * score_scale
        )
        dk_part = (
            jnp.einsum("kgqs,qkgd->skd", dscore_low, query_low, preferred_element_type=jnp.float32)
            * score_scale
        )
        dv_part = jnp.einsum(
            "kgqs,qkgd->skd", probs_low, dmix_low, preferred_element_type=jnp.float32
        )
        dk_rot, dv_sum = (
            lax.psum_scatter(
                dk_part.reshape(stream, kv_width).astype(jnp.bfloat16),
                "ctx",
                scatter_dimension=0,
                tiled=True,
            ).astype(jnp.float32),
            lax.psum_scatter(
                dv_part.reshape(stream, kv_width).astype(jnp.bfloat16),
                "ctx",
                scatter_dimension=0,
                tiled=True,
            ).astype(jnp.float32),
        )
        dq_low = (
            rotate_back(dq_rot.reshape(rows_own, HEADS, HEAD), cos_heads, sin_heads)
            .reshape(rows_own, HEADS * HEAD)
            .astype(jnp.bfloat16)
        )
        dk_low = (
            rotate_back(dk_rot.reshape(rows_own, KV_HEADS, HEAD), cos_heads, sin_heads)
            .reshape(rows_own, kv_width)
            .astype(jnp.bfloat16)
        )
        dv_low = dv_sum.astype(jnp.bfloat16)
        d_normed = jnp.einsum("te,de->td", dq_low, w_query, preferred_element_type=jnp.float32)
        d_normed = d_normed + jnp.einsum(
            "te,de->td", dk_low, w_key, preferred_element_type=jnp.float32
        )
        d_normed = d_normed + jnp.einsum(
            "te,de->td", dv_low, w_value, preferred_element_type=jnp.float32
        )
        d_input_part, d_gain_one = norm_pull(d_normed)
        input_grads.append((d_second + d_input_part).astype(jnp.bfloat16))
        new_pieces = [
            jnp.einsum("td,te->de", normed_low, dq_low, preferred_element_type=jnp.float32),
            jnp.einsum("td,te->de", normed_low, dk_low, preferred_element_type=jnp.float32),
            jnp.einsum("td,te->de", normed_low, dv_low, preferred_element_type=jnp.float32),
            jnp.einsum("td,te->de", mixed_low, branch_low, preferred_element_type=jnp.float32),
            jnp.sum(dq_low.astype(jnp.float32), axis=0),
            jnp.sum(dk_low.astype(jnp.float32), axis=0),
            jnp.sum(dv_low.astype(jnp.float32), axis=0),
            d_gain_one,
            d_gain_two,
        ]
        if grad_pieces is None:
            grad_pieces = new_pieces
        else:
            grad_pieces = [older + newer for older, newer in zip(grad_pieces, new_pieces)]
        kept_normed.append(two_low)
        kept_gate.append(gate_low)
        kept_up.append(up_low)
        kept_hidden.append(hidden_low)
        kept_cot.append(cot_low)
    attn_grad = lax.psum_scatter(
        pack_grads(grad_pieces, total_length), ("dp", "ctx"), scatter_dimension=0, tiled=True
    )
    stacked_all = jnp.stack(
        [
            jnp.concatenate(kept_gate, axis=0),
            jnp.concatenate(kept_up, axis=0),
            jnp.concatenate(kept_hidden, axis=0),
        ],
        axis=0,
    )
    columns_all = lax.all_to_all(stacked_all, "dp", split_axis=2, concat_axis=1, tiled=True)
    rows_pair = (jnp.concatenate(kept_normed, axis=0), jnp.concatenate(kept_cot, axis=0))
    sums_all = ffn_fold(
        columns_all,
        (
            lax.all_gather(rows_pair[0], "dp", axis=0, tiled=True),
            lax.all_gather(rows_pair[1], "dp", axis=0, tiled=True),
        ),
    )
    ffn_grad = lax.psum_scatter(
        sums_all.astype(jnp.bfloat16), "ctx", scatter_dimension=1, tiled=True
    ).astype(jnp.float32)
    return (jnp.stack(outputs, axis=0), jnp.stack(input_grads, axis=0), attn_grad, ffn_grad)


def solution(mesh):
    return jax.shard_map(
        per_device,
        mesh=mesh,
        in_specs=(
            P(None, ("dp", "ctx"), None),
            P("dp", None, None),
            P(("dp", "ctx")),
            P(None, ("dp", "ctx"), None),
            P(None, ("dp", "ctx"), None),
        ),
        out_specs=(
            P(None, ("dp", "ctx"), None),
            P(None, ("dp", "ctx"), None),
            P(("dp", "ctx")),
            P(None, ("dp", "ctx"), None),
        ),
        check_vma=False,
    )
```

profile of v0, /device:TPU:0, one launch (start us, length us, event | category | flops | bytes accessed | tf_op | source)
XLA Modules:
  0.0 817.3 jit_solution(1646062900324642096)
XLA Ops:
  21.9 65.8 %all-gather.12.cloned.1.call-done = bf16[32,1,57472]{2,1,0:T(2,128)(2,1)} async-done(((bf16[1,1,57472]{2,1,0:T(2,128)(2,1)}), bf16[32,1,57472]{2,1,0:T(2,128)(2,1)}) %all-gather.12.cloned.1.call-update) | async-done | bytes 3678224 | tf_op jit(solution)/shard_map/all_gather | solution.py:122
  87.7 79.7 %reduce.4 = bf16[32,57472]{1,0:T(8,128)(2,1)} reduce(bf16[32,1,57472]{2,1,0:T(2,128)(2,1)} %all-gather.12.cloned.1.call-done, bf16[]{:T(256)} %constant.61), dimensions={1}, to_apply=%all-gather.reduce_sub_computation | reduce | bytes 7356418 | tf_op jit(solution)/shard_map/all_gather | solution.py:122
  167.4 8.1 reshape.556
  186.2 5.6 all_gather.30
  194.2 5.9 all_gather.31
  215.4 5.7 all_gather.27
  230.8 5.7 all_gather.28
  261.7 6.1 fusion.3
  267.8 6.1 fusion.7
  274.0 7.0 multiply_convert_fusion.1
  281.0 5.6 fusion.1
  286.6 5.7 multiply_reduce_fusion.3
  292.4 6.3 fusion.2
  298.7 6.1 fusion.6
  304.8 7.0 multiply_convert_fusion
  311.8 5.5 fusion
  317.4 5.7 multiply_reduce_fusion.2
  383.4 8.5 %copy.195 = bf16[3,128,4864]{1,0,2:T(4,128)(2,1)} copy(bf16[3,128,4864]{2,1,0:T(8,128)(2,1)} %pad_maximum_fusion) | data formatting | bytes 7471104 | tf_op jit(solution)/shard_map/stack | solution.py:281
  411.6 5.6 reduce-scatter.16.cloned.1.call-done
  436.4 100.5 %all-to-all-done = bf16[3,128,4864]{1,0,2:T(4,128)(2,1)} async-done(((bf16[3,128,4864]{1,0,2:T(4,128)(2,1)}), bf16[3,128,4864]{1,0,2:T(4,128)(2,1)}, u32[]{:S(2)}, u32[]{:S(2)}) %all-to-all-start) | async-done | bytes 3735584 | tf_op jit(solution)/shard_map/all_to_all | solution.py:289
  549.3 12.2 %all-gather.10.cloned.1.call-done = bf16[1024,896]{1,0:T(8,128)(2,1)} async-done(((bf16[128,896]{1,0:T(8,128)(2,1)}), bf16[1024,896]{1,0:T(8,128)(2,1)}) %all-gather.10.cloned.1.call-update) | async-done | bytes 1835024 | tf_op jit(solution)/shard_map/all_gather | solution.py:295
  568.0 5.1 fusion.46
  580.0 155.1 %all-reduce.5.cloned.1.call-done = f32[1839104]{0:T(1024)} async-done(((f32[1839104]{0:T(1024)}), f32[1839104]{0:T(1024)}) %all-reduce.5.cloned.1.call-update) | async-done | bytes 7356432
  736.9 70.8 %all-reduce.7.cloned.1.call-done = bf16[3,608,896]{2,1,0:T(8,128)(2,1)} async-done(((bf16[3,608,896]{2,1,0:T(8,128)(2,1)}), bf16[3,608,896]{2,1,0:T(8,128)(2,1)}) %all-reduce.7.cloned.1.call-update) | async-done | bytes 3268624
  (405 shorter events, 205.2 us)
Async XLA Ops:
  7.2 13.3 %copy-start.6 = (bf16[2,64,896]{2,1,0:T(8,128)(2,1)S(1)}, bf16[2,64,896]{2,1,0:T(8,128)(2,1)}, u32[]{:S(2)}) copy-start(bf16[2,64,896]{2,1,0:T(8,128)(2,1)} %param.5) | copy-start | bytes 688132
  7.2 80.5 %all-gather.12.cloned.1.call-start = ((), (), s32[]{:S(2)}) async-start(), calls=%async_computation.10 | async-start | bytes 7586304 | tf_op jit(solution)/shard_map/all_gather | solution.py:122
  9.0 252.7 %all-gather.6.cloned.1.call-start = ((), (), s32[]{:S(2)}) async-start(), calls=%async_computation.5 | async-start | bytes 26966016 | tf_op jit(solution)/shard_map/all_gather | solution.py:123
  9.8 387.0 %reduce-scatter.12.cloned.1.call-start = ((), (), s32[]{:S(2)}) async-start(), calls=%async_computation.7 | async-start | bytes 81920 | tf_op jit(solution)/shard_map/reduce_scatter | solution.py:225
  16.8 177.3 %copy-start.54 = (f32[64,128]{1,0:T(8,128)}, f32[64,128]{1,0:T(8,128)S(1)}, u32[]{:S(2)}) copy-start(f32[64,128]{1,0:T(8,128)S(1)} %mul.576) | copy-start | bytes 98308
  19.6 147.8 %copy-start.58 = (f32[64,64]{0,1:T(8,128)}, f32[64,64]{0,1:T(8,128)S(1)}, u32[]{:S(2)}) copy-start(f32[64,64]{0,1:T(8,128)S(1)} %get-tuple-element.61) | copy-start | bytes 49156
  19.7 147.7 %copy-start.60 = (f32[64,64]{1,0:T(8,128)}, f32[64,64]{1,0:T(8,128)S(1)}, u32[]{:S(2)}) copy-start(f32[64,64]{1,0:T(8,128)S(1)} %copy.166) | copy-start | bytes 49156
  20.6 146.8 %copy-start.81 = (f32[64]{0:T(128)}, f32[64]{0:T(128)S(1)}, u32[]{:S(2)}) copy-start(f32[64]{0:T(128)S(1)} %get-tuple-element.14) | copy-start | bytes 772
  20.6 146.8 %copy-start.83 = (f32[64]{0:T(128)}, f32[64]{0:T(128)S(1)}, u32[]{:S(2)}) copy-start(f32[64]{0:T(128)S(1)} %get-tuple-element.15) | copy-start | bytes 772
  20.6 171.8 %copy-start.72 = (f32[64]{0:T(128)}, f32[64]{0:T(128)S(1)}, u32[]{:S(2)}) copy-start(f32[64]{0:T(128)S(1)} %fusion.117) | copy-start | bytes 772
  185.0 18.1 %copy-start.90 = (f32[128]{0:T(128)}, f32[128]{0:T(128)S(1)}, u32[]{:S(2)}) copy-start(f32[128]{0:T(128)S(1)} %get-tuple-element.28) | copy-start | bytes 1540
  209.0 13.6 %copy-start.91 = (f32[128]{0:T(128)S(1)}, f32[128]{0:T(128)}, u32[]{:S(2)}) copy-start(f32[128]{0:T(128)} %copy-done.90) | copy-start | bytes 1540
  261.0 56.3 %copy-start.85 = (f32[64]{0:T(128)}, f32[64]{0:T(128)S(1)}, u32[]{:S(2)}) copy-start(f32[64]{0:T(128)S(1)} %fusion.118) | copy-start | bytes 772
  333.1 68.5 %reduce-scatter.10.cloned.1.call-start = ((), (), s32[]{:S(2)}) async-start(), calls=%async_computation.6 | async-start | bytes 81920 | tf_op jit(solution)/shard_map/reduce_scatter | solution.py:225
  342.3 67.5 %reduce-scatter.14.cloned.1.call-start = ((), (), s32[]{:S(2)}) async-start(), calls=%async_computation.11 | async-start | bytes 81920
  345.9 71.3 %reduce-scatter.16.cloned.1.call-start = ((), (), s32[]{:S(2)}) async-start(), calls=%async_computation.12 | async-start | bytes 81920
  349.5 193.2 %all-gather.8.cloned.1.call-start = ((), (), s32[]{:S(2)}) async-start(), calls=%async_computation.8 | async-start | bytes 2064384 | tf_op jit(solution)/shard_map/all_gather | solution.py:294
  351.2 210.3 %all-gather.10.cloned.1.call-start = ((), (), s32[]{:S(2)}) async-start(), calls=%async_computation.9 | async-start | bytes 2064384 | tf_op jit(solution)/shard_map/all_gather | solution.py:295
  391.9 11.1 %copy-start.52 = (f32[64,64]{1,0:T(8,128)S(1)}, f32[64,64]{1,0:T(8,128)}, u32[]{:S(2)}) copy-start(f32[64,64]{1,0:T(8,128)} %copy.167) | copy-start | bytes 49156
  391.9 15.4 %copy-start.55 = (f32[64,128]{1,0:T(8,128)S(1)}, f32[64,128]{1,0:T(8,128)}, u32[]{:S(2)}) copy-start(f32[64,128]{1,0:T(8,128)} %copy-done.54) | copy-start | bytes 98308
  391.9 145.0 %all-to-all-start = ((bf16[3,128,4864]{1,0,2:T(4,128)(2,1)}), bf16[3,128,4864]{1,0,2:T(4,128)(2,1)}, u32[]{:S(2)}, u32[]{:S(2)}) async-start(bf16[3,128,4864]{1,0,2:T(4,128)(2,1)} %copy.195), calls=%async_computation.2 | async-start | bytes 9961472 | tf_op jit(solution)/shard_map/all_to_all | solution.py:289
  396.7 338.4 %all-reduce.5.cloned.1.call-start = ((), (), s32[]{:S(2)}) async-start(), calls=%async_computation.13 | async-start | bytes 14712832
  421.2 10.7 %copy-start.78 = (f32[896]{0:T(1024)S(1)}, f32[896]{0:T(1024)}, u32[]{:S(2)}) copy-start(f32[896]{0:T(1024)} %get-tuple-element.4) | copy-start | bytes 10756
  434.5 373.1 %all-reduce.7.cloned.1.call-start = ((), (), s32[]{:S(2)}) async-start(), calls=%async_computation.14 | async-start | bytes 6537216
  (82 other events, 292.0 us)
Sparse Core Ops, SparseCore 0:
  11.5 76.1 all-gather.11
  90.7 158.8 all-gather.5
  333.2 18.5 reduce-scatter.11
  354.2 19.3 reduce-scatter.9
  375.9 19.4 reduce-scatter.13
  397.7 19.4 reduce-scatter.15
  419.4 92.3 all-gather.7
  513.9 47.5 all-gather.9
  567.4 167.7 all-reduce.4
  737.4 70.2 all-reduce.6
where the time goes:
time: 829 us; the launch traced here: 817 us
  waiting for transfers between devices  411 us (50%)
  other arithmetic  130 us (16%)
  matrix products  126 us (15%)
  local copies, waits for them, and re-layouts  105 us (13%)
  blocking collectives  22.8 us (3%)
  between operations  16.6 us (2%)
    unnamed x14, waiting for transfers between devices  232 us
    all_to_all x1, waiting for transfers between devices, per_device(): lax.all_to_all(stacked_all, 'dp', split_axis=2, concat_axis=1, tiled=True)  101 us
    all_gather x1, other arithmetic, per_device(): lax.all_gather(attn_params, ('dp', 'ctx'), axis=0, tiled=True)  79.7 us
    all_gather x1, waiting for transfers between devices, per_device(): lax.all_gather(attn_params, ('dp', 'ctx'), axis=0, tiled=True)  65.8 us
    unnamed x203, local copies, waits for them, and re-layouts  33.9 us
  transfers between devices with their start and end apart: 11, of which 6 were waited for; matrix products, arithmetic and copies ran while one was open for 34% of the time, Pallas kernels for 0%

commit v1 on v0

v1 whole, which is shorter than its diff:
```python
import math

import jax
import jax.numpy as jnp
from jax import lax
from jax.sharding import Mesh
from jax.sharding import PartitionSpec as P

D = 896
HEADS = 14
KV_HEADS = 2
HEAD = 64


EPSILON = 1e-06
THETA = 1000000.0


def rms_norm(values, gain_vec):
    return (
        values * lax.rsqrt(jnp.mean(values * values, axis=-1, keepdims=True) + EPSILON) * gain_vec
    )


def rotate(values, cosine, sine_table):
    half_width = values.shape[-1] // 2
    turned = jnp.concatenate([-values[..., half_width:], values[..., :half_width]], axis=-1)
    return values * cosine + turned * sine_table


def rotate_back(incoming, cosine, sine_table):
    scaled = incoming * sine_table
    half_width = incoming.shape[-1] // 2
    turned = jnp.concatenate([scaled[..., half_width:], -scaled[..., :half_width]], axis=-1)
    return incoming * cosine + turned


def geometry(seq_lens, slot_ids):
    seq_ends = jnp.cumsum(seq_lens)
    seq_starts = seq_ends - seq_lens
    filled = seq_ends[-1]
    numbers = jnp.arange(seq_lens.shape[0], dtype=jnp.int32)
    segment = jnp.sum((slot_ids[:, None] >= seq_ends[None, :]).astype(jnp.int32), axis=1)
    seq_begin = jnp.sum(
        jnp.where(segment[:, None] == numbers[None, :], seq_starts[None, :], 0), axis=1
    )
    inside = slot_ids < filled
    segment = jnp.where(inside, segment, seq_lens.shape[0] + slot_ids)
    position = jnp.where(inside, slot_ids - seq_begin, 0)
    return (segment, position)


def rotary_tables(position):
    half_width = HEAD // 2
    frequency = jnp.power(THETA, -(jnp.arange(half_width, dtype=jnp.float32) * 2.0 / HEAD))
    angles = position.astype(jnp.float32)[:, None] * frequency[None, :]
    cosine = jnp.concatenate([jnp.cos(angles), jnp.cos(angles)], axis=-1)
    sine_table = jnp.concatenate([jnp.sin(angles), jnp.sin(angles)], axis=-1)
    return (cosine, sine_table)


def unpack(flat_params):
    kv_width = KV_HEADS * HEAD
    shapes_list = [
        (D, D),
        (D, kv_width),
        (D, kv_width),
        (D, D),
        (D,),
        (kv_width,),
        (kv_width,),
        (D,),
        (D,),
    ]
    pieces = []
    offset = 0
    for piece_shape in shapes_list:
        entries = math.prod(piece_shape)
        pieces.append(flat_params[offset : offset + entries].reshape(piece_shape))
        offset += entries
    return pieces


def pack_grads(pieces, total_length):
    flat_grad = jnp.concatenate([piece.reshape(-1) for piece in pieces])
    padding = total_length - flat_grad.shape[0]
    return jnp.concatenate([flat_grad, jnp.zeros((padding,), jnp.float32)])


def per_device(tokens, seq_lengths, attn_params, ffn_weight, out_grad):
    micro_count, rows_own = tokens.shape[0], tokens.shape[1]
    stream = rows_own * lax.axis_size("ctx")
    rows = micro_count * rows_own
    groups = HEADS // KV_HEADS
    kv_width = KV_HEADS * HEAD
    score_scale = HEAD ** (-0.5)
    units = ffn_weight.shape[1]
    far = lax.axis_size("hi")
    devices = far * lax.axis_size("lo") * lax.axis_size("ctx")
    total_length = attn_params.shape[0] * devices
    f32, bf16 = jnp.float32, jnp.bfloat16

    cot_low = out_grad.reshape(rows, D)
    ffn_all = lax.all_gather(ffn_weight.reshape(3 * units, D), "hi", axis=0, tiled=False)
    attn_all = lax.all_gather(
        attn_params.reshape(-1, 128), ("hi", "lo", "ctx"), axis=0, tiled=False
    ).reshape(-1)
    cot_all = lax.all_gather(cot_low, ("lo", "ctx"), axis=0, tiled=True)
    w_query, w_key, w_value, w_out, b_query, b_key, b_value, gain_one, gain_two = unpack(attn_all)
    w_qkv = jnp.concatenate([w_query, w_key, w_value], axis=1)
    b_qkv = jnp.concatenate([b_query, b_key, b_value], axis=0).astype(f32)

    slot_ids = jnp.arange(stream, dtype=jnp.int32)
    first_slot = lax.axis_index("ctx") * rows_own
    own_slots = first_slot + jnp.arange(rows_own, dtype=jnp.int32)
    segment, position = jax.vmap(geometry, in_axes=(0, None))(seq_lengths[0], slot_ids)
    own_segment = lax.dynamic_slice_in_dim(segment, first_slot, rows_own, axis=1)
    own_position = lax.dynamic_slice_in_dim(position, first_slot, rows_own, axis=1)
    cosine, sine_table = rotary_tables(own_position.reshape(-1))
    cos_heads, sin_heads = cosine[:, None, :], sine_table[:, None, :]
    allowed = (own_segment[:, :, None] == segment[:, None, :]) & (
        slot_ids[None, None, :] <= own_slots[None, :, None]
    )

    x_float = tokens.reshape(rows, D).astype(f32)
    normed, norm_pull = jax.vjp(rms_norm, x_float, gain_one.astype(f32))
    normed_low = normed.astype(bf16)
    qkv = jnp.dot(normed_low, w_qkv, preferred_element_type=f32) + b_qkv
    query_pre, key_pre, value_pre = jnp.split(qkv, [D, D + kv_width], axis=1)
    query_low = rotate(query_pre.reshape(rows, HEADS, HEAD), cos_heads, sin_heads).astype(bf16)
    key_low = rotate(key_pre.reshape(rows, KV_HEADS, HEAD), cos_heads, sin_heads).astype(bf16)
    kv_low = jnp.concatenate([key_low.reshape(rows, kv_width), value_pre.astype(bf16)], axis=1)
    kv_all = lax.all_gather(
        kv_low.reshape(micro_count, rows_own, 2 * kv_width), "ctx", axis=1, tiled=True
    )
    kv_all = kv_all.reshape(micro_count, stream, 2, KV_HEADS, HEAD)
    keys_all, values_all = kv_all[:, :, 0], kv_all[:, :, 1]
    query_low = query_low.reshape(micro_count, rows_own, KV_HEADS, groups, HEAD)
    scores = (
        jnp.einsum("mqkgd,mskd->mkgqs", query_low, keys_all, preferred_element_type=f32)
        * score_scale
    )
    scores = jnp.where(allowed[:, None, None], scores, -1e30)
    soft_probs = jax.nn.softmax(scores, axis=-1)
    probs_low = soft_probs.astype(bf16)
    mixed = jnp.einsum("mkgqs,mskd->mqkgd", probs_low, values_all, preferred_element_type=f32)
    mixed_low = mixed.reshape(rows, HEADS * HEAD).astype(bf16)
    second = x_float + jnp.dot(mixed_low, w_out, preferred_element_type=f32)
    normed_two, norm_two_pull = jax.vjp(rms_norm, second, gain_two.astype(f32))
    two_low = normed_two.astype(bf16)

    two_all = lax.all_gather(two_low, ("lo", "ctx"), axis=0, tiled=True)
    ffn_all = ffn_all.reshape(far, 3, units, D).transpose(1, 0, 2, 3).reshape(3, far * units, D)
    w_gate, w_up, w_down = ffn_all[0], ffn_all[1], ffn_all[2]
    d_hidden = jnp.einsum("td,fd->tf", cot_all, w_down, preferred_element_type=f32)
    gate_out = jnp.einsum("td,fd->tf", two_all, w_gate, preferred_element_type=f32)
    up_out = jnp.einsum("td,fd->tf", two_all, w_up, preferred_element_type=f32)
    sig = jax.nn.sigmoid(gate_out)
    silu = gate_out * sig
    hidden_low = (silu * up_out).astype(bf16)
    gate_low = (d_hidden * up_out * sig * (1.0 + gate_out * (1.0 - sig))).astype(bf16)
    up_low = (d_hidden * silu).astype(bf16)
    d_two_part = jnp.einsum("tf,fd->td", gate_low, w_gate, preferred_element_type=f32)
    d_two_part += jnp.einsum("tf,fd->td", up_low, w_up, preferred_element_type=f32)
    d_two = lax.psum_scatter(
        d_two_part.astype(bf16), ("lo", "ctx"), scatter_dimension=0, tiled=True
    ).astype(f32)
    out_part = jnp.einsum("tf,fd->td", hidden_low, w_down, preferred_element_type=f32)
    out_sum = lax.psum_scatter(
        out_part.astype(bf16), ("lo", "ctx"), scatter_dimension=0, tiled=True
    ).astype(f32)
    result = (second + out_sum).astype(bf16)
    grad_gate = jnp.einsum("tf,td->fd", gate_low, two_all, preferred_element_type=f32)
    grad_up = jnp.einsum("tf,td->fd", up_low, two_all, preferred_element_type=f32)
    grad_down = jnp.einsum("tf,td->fd", hidden_low, cot_all, preferred_element_type=f32)
    ffn_part = jnp.stack([grad_gate, grad_up, grad_down], axis=0).astype(bf16)
    ffn_grad = lax.psum_scatter(ffn_part, "hi", scatter_dimension=1, tiled=True).astype(f32)

    d_second_part, d_gain_two = norm_two_pull(d_two)
    d_second = cot_low.astype(f32) + d_second_part
    branch_low = d_second.astype(bf16)
    d_mixed = jnp.einsum("te,de->td", branch_low, w_out, preferred_element_type=f32)
    dmix_low = d_mixed.astype(bf16).reshape(micro_count, rows_own, KV_HEADS, groups, HEAD)
    d_probs = jnp.einsum("mqkgd,mskd->mkgqs", dmix_low, values_all, preferred_element_type=f32)
    row_delta = jnp.sum(soft_probs * d_probs, axis=-1, keepdims=True)
    dscore_low = (soft_probs * (d_probs - row_delta)).astype(bf16)
    dq_rot = (
        jnp.einsum("mkgqs,mskd->mqkgd", dscore_low, keys_all, preferred_element_type=f32)
        * score_scale
    )
    dk_part = (
        jnp.einsum("mkgqs,mqkgd->mskd", dscore_low, query_low, preferred_element_type=f32)
        * score_scale
    )
    dv_part = jnp.einsum("mkgqs,mqkgd->mskd", probs_low, dmix_low, preferred_element_type=f32)
    dkv_part = jnp.concatenate(
        [
            dk_part.reshape(micro_count, stream, kv_width),
            dv_part.reshape(micro_count, stream, kv_width),
        ],
        axis=2,
    )
    dkv = lax.psum_scatter(dkv_part.astype(bf16), "ctx", scatter_dimension=1, tiled=True)
    dkv = dkv.reshape(rows, 2 * kv_width)
    dq_low = (
        rotate_back(dq_rot.reshape(rows, HEADS, HEAD), cos_heads, sin_heads)
        .reshape(rows, HEADS * HEAD)
        .astype(bf16)
    )
    dk_rot = dkv[:, :kv_width].astype(f32).reshape(rows, KV_HEADS, HEAD)
    dk_low = rotate_back(dk_rot, cos_heads, sin_heads).reshape(rows, kv_width).astype(bf16)
    d_qkv = jnp.concatenate([dq_low, dk_low, dkv[:, kv_width:]], axis=1)
    d_normed = jnp.einsum("te,de->td", d_qkv, w_qkv, preferred_element_type=f32)
    d_input_part, d_gain_one = norm_pull(d_normed)
    input_grad = (d_second + d_input_part).astype(bf16)
    grad_qkv = jnp.einsum("td,te->de", normed_low, d_qkv, preferred_element_type=f32)
    grad_out = jnp.einsum("td,te->de", mixed_low, branch_low, preferred_element_type=f32)
    grad_bias = jnp.sum(d_qkv.astype(f32), axis=0)
    pieces = [
        grad_qkv[:, :D],
        grad_qkv[:, D : D + kv_width],
        grad_qkv[:, D + kv_width :],
        grad_out,
        grad_bias,
        d_gain_one,
        d_gain_two,
    ]
    flat_grad = pack_grads(pieces, total_length)
    attn_grad = lax.psum_scatter(
        flat_grad.astype(bf16).reshape(devices, -1, 128),
        ("hi", "lo", "ctx"),
        scatter_dimension=0,
        tiled=True,
    ).astype(f32)
    shape = tokens.shape
    return (result.reshape(shape), input_grad.reshape(shape), attn_grad.reshape(-1), ffn_grad)


def solution(mesh):
    grid = mesh.devices
    split = Mesh(grid.reshape(grid.shape[0] // 2, 2, grid.shape[1]), ("hi", "lo", "ctx"))
    every = ("hi", "lo", "ctx")
    return jax.shard_map(
        per_device,
        mesh=split,
        in_specs=(
            P(None, every, None),
            P(("hi", "lo"), None, None),
            P(every),
            P(None, every, None),
            P(None, every, None),
        ),
        out_specs=(
            P(None, every, None),
            P(None, every, None),
            P(every),
            P(None, every, None),
        ),
        check_vma=False,
    )
```

time: 829 us -> 562 us (0.68); the launches traced: 817 us -> 560 us
  other arithmetic: 130 us -> 26.7 us
  matrix products: 126 us -> 49.7 us
  local copies, waits for them, and re-layouts: 105 us -> 62.4 us
  blocking collectives: 22.8 us -> 6.24 us
  waiting for transfers between devices: 411 us -> 399 us
    all_to_all x1 -> x0, waiting for transfers between devices: 101 us -> none  [per_device(): lax.all_to_all(stacked_all, 'dp', split_axis=2, concat_axis=1, tiled=True)]
    all_gather x1 -> x0, other arithmetic: 79.7 us -> none  [per_device(): lax.all_gather(attn_params, ('dp', 'ctx'), axis=0, tiled=True)]
    dot_general x51 -> x20, matrix products: 126 us -> 46.6 us  [the longest x1 6.45 us: per_device(): jnp.einsum('td,fd->tf', cot_all, w_down, preferred_element_type=f32)]
    reduce_scatter x2 -> x3, waiting for transfers between devices: 0.02 us -> 75.2 us  [the longest x1 41.8 us: per_device(): lax.psum_scatter(out_part.astype(bf16), ('lo', 'ctx'), scatter_dimension=...]
    all_gather x4, waiting for transfers between devices: 78.1 us -> 121 us  [the longest x1 58.4 us: per_device(): lax.all_gather(attn_params.reshape(-1, 128), ('hi', 'lo', 'ctx'), axis=0,...]
    unnamed x14 -> x11, waiting for transfers between devices: 232 us -> 202 us
    unnamed x203 -> x76, local copies, waits for them, and re-layouts: 33.9 us -> 13.5 us
    all_gather x4 -> x1, blocking collectives: 22.8 us -> 6.24 us  [per_device(): lax.all_gather(kv_low.reshape(micro_count, rows_own, 2 * kv_width), 'ctx'...]
  transfers between devices with their start and end apart: 11 -> 9, of which waited for: 6 -> 9; matrix products, arithmetic and copies ran while one was open for 34% -> 20% of each run, Pallas kernels for 0% -> 0%
where the time goes in v1:
time: 562 us; the launch traced here: 560 us
  waiting for transfers between devices  399 us (71%)
  local copies, waits for them, and re-layouts  62.4 us (11%)
  matrix products  49.7 us (9%)
  other arithmetic  26.7 us (5%)
  between operations  15.1 us (3%)
  blocking collectives  6.24 us (1%)
    unnamed x11, waiting for transfers between devices  202 us
    all_gather x1, waiting for transfers between devices, per_device(): lax.all_gather(attn_params.reshape(-1, 128), ('hi', 'lo', 'ctx'), axis=0,...  58.4 us
    reduce_scatter x1, waiting for transfers between devices, per_device(): lax.psum_scatter(out_part.astype(bf16), ('lo', 'ctx'), scatter_dimension=...  41.8 us
    reduce_scatter x1, waiting for transfers between devices, per_device(): lax.psum_scatter(d_two_part.astype(bf16), ('lo', 'ctx'), scatter_dimensio...  28.1 us
    all_gather x1, waiting for transfers between devices, per_device(): two_all = lax.all_gather(two_low, ('lo', 'ctx'), axis=0, tiled=True)  24.4 us
    all_gather x1, waiting for transfers between devices, per_device(): cot_all = lax.all_gather(cot_low, ('lo', 'ctx'), axis=0, tiled=True)  20.7 us
    all_gather x1, waiting for transfers between devices, per_device(): lax.all_gather(ffn_weight.reshape(3 * units, D), 'hi', axis=0, tiled=False)  17.8 us
    unnamed x76, local copies, waits for them, and re-layouts  13.5 us
  transfers between devices with their start and end apart: 9, of which 9 were waited for; matrix products, arithmetic and copies ran while one was open for 20% of the time, Pallas kernels for 0%

profile of v1, /device:TPU:0, one launch (start us, length us, event | category | flops | bytes accessed | tf_op | source)
XLA Modules:
  0.0 560.0 jit_solution(8767131351978076011)
XLA Ops:
  15.9 58.4 %all-gather.5.cloned.1.call-done = bf16[32,449,128]{2,1,0:T(8,128)(2,1)} async-done(((bf16[1,449,128]{2,1,0:T(8,128)(2,1)}), bf16[32,449,128]{2,1,0:T(8,128)(2,1)}) %all-gather.5.cloned.1.call-update) | async-done | bytes 3678224 | tf_op jit(solution)/shard_map/all_gather | solution.py:105
  74.3 4.9 reshape.301
  83.9 5.0 slice.93
  100.3 6.2 %all_gather.16 = bf16[2,256,256]{2,0,1:T(2,128)(2,1)} all-gather(bf16[2,64,256]{2,0,1:T(2,128)(2,1)S(1)} %pad_maximum_fusion.7), channel_id=1, replica_groups=mesh['hi'=4,'lo'=2,'ctx'=4] {'ctx'}, dimensions={1}, use_global_device_ids=true | all-gather | bytes 327680 | tf_op jit(solution)/shard_map/all_gather | solution.py:133
  111.0 3.1 fusion.66
  122.4 17.8 %all-gather.9.cloned.1.call-done = bf16[4,456,896]{2,1,0:T(8,128)(2,1)} async-done(((bf16[1,456,896]{2,1,0:T(8,128)(2,1)}), bf16[4,456,896]{2,1,0:T(8,128)(2,1)}) %all-gather.9.cloned.1.call-update) | async-done | bytes 3268624 | tf_op jit(solution)/shard_map/all_gather | solution.py:104
  140.3 3.5 fusion.62
  143.7 24.4 %all-gather.7.cloned.1.call-done = bf16[1024,896]{1,0:T(8,128)(2,1)} async-done(((bf16[128,896]{1,0:T(8,128)(2,1)}), bf16[1024,896]{1,0:T(8,128)(2,1)}) %all-gather.7.cloned.1.call-update) | async-done | bytes 1835024 | tf_op jit(solution)/shard_map/all_gather | solution.py:152
  168.2 4.9 fusion.69
  173.1 3.0 fusion.70
  176.0 20.7 %all-gather.11.cloned.1.call-done = bf16[1024,896]{1,0:T(8,128)(2,1)} async-done(((bf16[128,896]{1,0:T(8,128)(2,1)}), bf16[1024,896]{1,0:T(8,128)(2,1)}) %all-gather.11.cloned.1.call-update) | async-done | bytes 1835024 | tf_op jit(solution)/shard_map/all_gather | solution.py:108
  196.7 6.5 %multiply_convert_fusion = (bf16[1024,608]{0,1:T(8,128)(2,1)S(1)}, bf16[1024,608]{0,1:T(8,128)(2,1)S(1)}, bf16[1024,608]{0,1:T(8,128)(2,1)}) fusion(f32[1024,608]{0,1:T(8,128)} %fusion.69, f32[1024,608]{0,1:T(8,128)} %fusion.70, bf16[1024,896]{1,0:T(8,128)(2,1)} %all-gather.11.cloned.1.call-done, bf16[608,896]{1,0:T(8,128)(2,1)S(1)} %bitcast.181), kind=kOutput, calls=%fused_computation.5 | convolution fusion | flops 1125023744 | bytes 11640832 | tf_op jit(solution)/shard_map/td,fd->tf/dot_general | solution.py:155
  205.3 3.2 add_convert_fusion
  208.5 4.3 convolution_convert_fusion.1
  213.1 4.5 fusion.6
  220.2 28.1 %reduce-scatter.10.cloned.1.call-done = bf16[128,896]{1,0:T(8,128)(2,1)} async-done(((bf16[1024,896]{1,0:T(8,128)(2,1)}), bf16[128,896]{1,0:T(8,128)(2,1)}) %reduce-scatter.10.cloned.1.call-update) | async-done | bytes 229392 | tf_op jit(solution)/shard_map/reduce_scatter | solution.py:165
  249.4 41.8 %reduce-scatter.8.cloned.1.call-done = bf16[128,896]{1,0:T(8,128)(2,1)} async-done(((bf16[1024,896]{1,0:T(8,128)(2,1)}), bf16[128,896]{1,0:T(8,128)(2,1)}) %reduce-scatter.8.cloned.1.call-update) | async-done | bytes 229392 | tf_op jit(solution)/shard_map/reduce_scatter | solution.py:169
  300.0 3.5 fusion.8
  314.9 5.3 reduce-scatter.12.cloned.1.call-done
  324.2 4.2 reshape.319
  328.4 2.8 constant_dynamic-update-slice_fusion.1
  341.6 4.9 convert_element_type.159
  348.3 99.5 %all-reduce.4.cloned.1.call-done = bf16[3,608,896]{2,1,0:T(8,128)(2,1)} async-done(((bf16[3,608,896]{2,1,0:T(8,128)(2,1)}), bf16[3,608,896]{2,1,0:T(8,128)(2,1)}) %all-reduce.4.cloned.1.call-update) | async-done | bytes 3268624
  451.1 100.8 %reduce-scatter.14.cloned.1.call-done = bf16[1,449,128]{2,1,0:T(8,128)(2,1)} async-done(((bf16[32,449,128]{2,1,0:T(8,128)(2,1)}), bf16[1,449,128]{2,1,0:T(8,128)(2,1)}) %reduce-scatter.14.cloned.1.call-update) | async-done | bytes 114960
  (195 shorter events, 83.6 us)
Async XLA Ops:
  7.2 67.1 %all-gather.5.cloned.1.call-start = ((), (), s32[]{:S(2)}) async-start(), calls=%async_computation.4 | async-start | bytes 3852288 | tf_op jit(solution)/shard_map/all_gather | solution.py:105
  7.9 132.4 %all-gather.9.cloned.1.call-start = ((), (), s32[]{:S(2)}) async-start(), calls=%async_computation.6 | async-start | bytes 4085760 | tf_op jit(solution)/shard_map/all_gather | solution.py:104
  8.6 159.5 %all-gather.7.cloned.1.call-start = ((), (), s32[]{:S(2)}) async-start(), calls=%async_computation.5 | async-start | bytes 2064384 | tf_op jit(solution)/shard_map/all_gather | solution.py:152
  83.8 6.4 %copy-start.1 = (bf16[2,64,896]{2,1,0:T(8,128)(2,1)S(1)}, bf16[2,64,896]{2,1,0:T(8,128)(2,1)}, u32[]{:S(2)}) copy-start(bf16[2,64,896]{2,1,0:T(8,128)(2,1)} %param.5) | copy-start | bytes 688132
  83.9 7.7 %copy-start.5 = (bf16[896,896]{1,0:T(8,128)(2,1)S(1)}, bf16[896,896]{1,0:T(8,128)(2,1)}, u32[]{:S(2)}) copy-start(bf16[896,896]{1,0:T(8,128)(2,1)} %reshape.302) | copy-start | bytes 4816900
  94.0 3.6 slice-start
  97.5 10.9 %copy-start.19 = (f32[2,64,64]{1,0,2:T(2,128)S(1)}, f32[2,64,64]{1,0,2:T(2,128)}, u32[]{:S(2)}) copy-start(f32[2,64,64]{1,0,2:T(2,128)} %get-tuple-element.43) | copy-start | bytes 98308
  97.5 10.9 %copy-start.20 = (f32[2,64,64]{1,0,2:T(2,128)S(1)}, f32[2,64,64]{1,0,2:T(2,128)}, u32[]{:S(2)}) copy-start(f32[2,64,64]{1,0,2:T(2,128)} %get-tuple-element.44) | copy-start | bytes 98308
  98.5 12.5 %copy-start.24 = (pred[2,64,256]{2,1,0:T(8,128)(4,1)S(1)}, pred[2,64,256]{2,1,0:T(8,128)(4,1)}, u32[]{:S(2)}) copy-start(pred[2,64,256]{2,1,0:T(8,128)(4,1)} %compare_and_fusion) | copy-start | bytes 98308
  121.6 75.1 %all-gather.11.cloned.1.call-start = ((), (), s32[]{:S(2)}) async-start(), calls=%async_computation.8 | async-start | bytes 2064384 | tf_op jit(solution)/shard_map/all_gather | solution.py:108
  122.2 126.1 %reduce-scatter.10.cloned.1.call-start = ((), (), s32[]{:S(2)}) async-start(), calls=%async_computation.9 | async-start | bytes 2064384 | tf_op jit(solution)/shard_map/reduce_scatter | solution.py:165
  168.2 4.9 copy-start.9
  168.2 4.9 copy-start.25
  196.7 6.5 %copy-start.11 = (bf16[1,4,152,896]{3,2,0,1:T(8,128)(2,1)S(1)}, bf16[1,4,152,896]{3,2,0,1:T(8,128)(2,1)}, u32[]{:S(2)}) copy-start(bf16[1,4,152,896]{3,2,0,1:T(8,128)(2,1)} %get-tuple-element.19) | copy-start | bytes 3268612
  208.5 82.8 %reduce-scatter.8.cloned.1.call-start = ((), (), s32[]{:S(2)}) async-start(), calls=%async_computation.7 | async-start | bytes 2064384 | tf_op jit(solution)/shard_map/reduce_scatter | solution.py:169
  212.8 107.3 %reduce-scatter.12.cloned.1.call-start = ((), (), s32[]{:S(2)}) async-start(), calls=%async_computation.10 | async-start | bytes 327680 | tf_op jit(solution)/shard_map/reduce_scatter | solution.py:203
  213.1 4.6 copy-start.26
  213.1 4.6 copy-start.31
  217.7 73.6 %copy-start.13 = (bf16[2,64,896]{2,1,0:T(8,128)(2,1)S(1)}, bf16[2,64,896]{2,1,0:T(8,128)(2,1)}, u32[]{:S(2)}) copy-start(bf16[2,64,896]{2,1,0:T(8,128)(2,1)} %param.9) | copy-start | bytes 688132
  300.0 147.9 %all-reduce.4.cloned.1.call-start = ((), (), s32[]{:S(2)}) async-start(), calls=%async_computation.11 | async-start | bytes 6537216
  305.8 246.2 %reduce-scatter.14.cloned.1.call-start = ((), (), s32[]{:S(2)}) async-start(), calls=%async_computation.12 | async-start | bytes 3852288
  311.1 3.7 copy-start.4
  328.4 4.3 copy-start
  346.5 103.8 %copy-start.29 = (f32[128]{0:T(128)S(1)}, f32[128]{0:T(128)}, u32[]{:S(2)}) copy-start(f32[128]{0:T(128)} %copy-done.28) | copy-start | bytes 1540
  (19 other events, 36.1 us)
Sparse Core Ops, SparseCore 0:
  10.9 63.2 all-gather.4
  75.8 64.3 all-gather.8
  142.7 25.4 all-gather.6
  169.9 26.7 all-gather.10
  208.6 39.6 reduce-scatter.9
  251.5 39.6 reduce-scatter.7
  300.1 19.9 reduce-scatter.11
  322.7 125.1 all-reduce.3
  454.5 97.4 reduce-scatter.13

commit v2 on v1

--- a/solution.py
+++ b/solution.py
@@ -1,8 +1,10 @@
-import math
+import functools
 
 import jax
 import jax.numpy as jnp
 from jax import lax
+from jax.experimental import pallas as pl
+from jax.experimental.pallas import tpu as pltpu
 from jax.sharding import Mesh
 from jax.sharding import PartitionSpec as P
 
@@ -59,32 +61,343 @@
     return (cosine, sine_table)
 
 
-def unpack(flat_params):
-    kv_width = KV_HEADS * HEAD
-    shapes_list = [
-        (D, D),
-        (D, kv_width),
-        (D, kv_width),
-        (D, D),
-        (D,),
-        (kv_width,),
-        (kv_width,),
-        (D,),
-        (D,),
+QKV = (HEADS + 2 * KV_HEADS) * HEAD
+LANES = 128
+W = D // LANES
+MATRIX_ROWS = 2 * D * W + 2 * D * KV_HEADS * HEAD // LANES
+SMALL_ROWS = 24
+MESH = pl.DeviceIdType.MESH
+
+
+class Place:
+    def __init__(self, ctx):
+        self.ctx = ctx
+        self.hi = lax.axis_index("hi")
+        self.lo = lax.axis_index("lo")
+        self.c = lax.axis_index("ctx")
+        self.sib = self.c + 1 - 2 * lax.rem(self.c, 2)
+        self.rels = [(a, b) for a in range(2) for b in range(ctx // 2)]
+        self.n = len(self.rels)
+
+    def to(self, r, c=None):
+        a, b = self.rels[r]
+        c = self.c if c is None else c
+        return lax.rem(self.lo + a, 2), lax.rem(c + 2 * b, self.ctx)
+
+    def source(self, r, c=None):
+        a, b = self.rels[r]
+        c = self.c if c is None else c
+        return lax.rem(self.lo + 2 - a, 2), lax.rem(c + self.ctx - 2 * b, self.ctx)
+
+    def slot(self, pair):
+        return pair[0] * self.ctx + pair[1]
+
+    def cube(self):
+        return [(self.hi,) + self.to(r) for r in range(1, self.n)] + [self.sibling()]
+
+    def sibling(self):
+        return (self.hi, self.lo, self.sib)
+
+
+def greet(devices):
+    barrier = pltpu.get_barrier_semaphore()
+    for device in devices:
+        pl.semaphore_signal(barrier, inc=1, device_id=device, device_id_type=MESH)
+    pl.semaphore_wait(barrier, len(devices))
+
+
+def remote(src, dst, send, recv, device):
+    return pltpu.make_async_remote_copy(
+        src_ref=src, dst_ref=dst, send_sem=send, recv_sem=recv,
+        device_id=device, device_id_type=MESH,
+    )
+
+
+class CubeGather:
+    def __init__(self, at, own, out, sems, aim=lambda out, slot: out.at[slot]):
+        self.at, self.own, self.out, self.aim = at, own, out, aim
+        self.send1, self.recv1, self.send2, self.recv2 = sems
+        self.started = []
+
+    def go(self, copy):
+        copy.start()
+        self.started.append(copy)
+
+    def push(self):
+        at = self.at
+        mine = self.aim(self.out, at.slot((at.lo, at.c)))
+        for r in range(1, at.n):
+            self.go(remote(self.own, mine, self.send1.at[r], self.recv1.at[r], (at.hi,) + at.to(r)))
+        self.go(remote(self.own, mine, self.send2.at[0], self.recv2.at[0], at.sibling()))
+
+    def forward(self):
+        at = self.at
+        for r in range(1, at.n):
+            here = self.aim(self.out, at.slot(at.source(r)))
+            remote(here, here, self.send1.at[r], self.recv1.at[r], (at.hi,) + at.to(r)).wait_recv()
+            self.go(remote(here, here, self.send2.at[r], self.recv2.at[r], at.sibling()))
+
+    def finish(self):
+        at = self.at
+        for r in range(at.n):
+            here = self.aim(self.out, at.slot(at.source(r, at.sib)))
+            remote(here, here, self.send2.at[r], self.recv2.at[r], at.sibling()).wait_recv()
+        for copy in self.started:
+            copy.wait_send()
+
+
+class CubeScatter:
+    def __init__(self, at, part, bufs, sems):
+        self.at, self.part = at, part
+        self.buf1, self.tmp, self.buf2 = bufs
+        self.send1, self.recv1, self.send2, self.recv2 = sems
+        self.started = []
+
+    def go(self, copy):
+        copy.start()
+        self.started.append(copy)
+
+    def push(self):
+        at = self.at
+        for r in list(range(1, at.n)) + [0]:
+            there = at.slot(at.to(r, at.sib))
+            self.go(remote(self.part.at[there], self.buf1.at[r], self.send1.at[r], self.recv1.at[r], at.sibling()))
+
+    def arrived(self, r):
+        at = self.at
+        remote(self.buf1.at[r], self.buf1.at[r], self.send1.at[r], self.recv1.at[r], at.sibling()).wait_recv()
+        mine = self.part[at.slot(at.to(r))].astype(jnp.float32)
+        return mine + self.buf1[r].astype(jnp.float32)
+
+    def forward(self):
+        at = self.at
+        for r in range(1, at.n):
+            self.tmp[r] = self.arrived(r).astype(jnp.bfloat16)
+            self.go(remote(self.tmp.at[r], self.buf2.at[r], self.send2.at[r], self.recv2.at[r], (at.hi,) + at.to(r)))
+
+    def finish(self):
+        at = self.at
+        total = self.arrived(0)
+        for r in range(1, at.n):
+            remote(self.buf2.at[r], self.buf2.at[r], self.send2.at[r], self.recv2.at[r], (at.hi,) + at.to(r)).wait_recv()
+            total = total + self.buf2[r].astype(jnp.float32)
+        return total
+
+    def drain(self):
+        for copy in self.started:
+            copy.wait_send()
+
+
+def params_kernel(far, ctx, shard, pad, *refs):
+    attn_ref, cot_ref, qkv_ref, wout_ref, small_ref, cots_ref, held, flat = refs[:8]
+    send_z, recv_z = refs[8:10]
+    piece_sems, cot_sems = refs[10:14], refs[14:18]
+    at = Place(ctx)
+    beyond = [(lax.rem(at.hi + h, far), at.lo, at.c) for h in range(1, far)]
+    greet(at.cube() + beyond)
+    mine = at.slot((at.lo, at.c))
+    for h in range(1, far):
+        remote(attn_ref, held.at[mine, at.hi], send_z.at[h], recv_z.at[h], beyond[h - 1]).start()
+    gathers = []
+    for h in range(far):
+        origin = lax.rem(at.hi + far - h, far)
+        own = attn_ref if h == 0 else held.at[mine, origin]
+        if h:
+            remote(own, own, send_z.at[h], recv_z.at[h], beyond[h - 1]).wait_recv()
+        gather = CubeGather(
+            at, own, held, [s.at[h] for s in piece_sems],
+            lambda out, slot, origin=origin: out.at[slot, origin],
+        )
+        gather.push()
+        gathers.append(gather)
+    held[mine, at.hi] = attn_ref[...]
+    cots = CubeGather(at, cot_ref, cots_ref, cot_sems)
+    cots.push()
+    cots_ref[mine] = cot_ref[...]
+    for gather in gathers:
+        gather.forward()
+    cots.forward()
+    for gather in gathers:
+        gather.finish()
+    for g in range(0, far * 2 * ctx):
+        block = held[g % (2 * ctx), g // (2 * ctx)].astype(jnp.float32)
+        flat[pl.ds(g * shard, pad), :] = block
+    for j in range(W):
+        cols = pl.ds(j * LANES, LANES)
+        qkv_ref[:, cols] = flat[pl.ds(j, D, stride=W), :].astype(jnp.bfloat16)
+        wout_ref[:, cols] = flat[pl.ds(D * W + 2 * D + j, D, stride=W), :].astype(jnp.bfloat16)
+    for j in range(2):
+        cols = pl.ds(D + j * LANES, LANES)
+        qkv_ref[:, cols] = flat[pl.ds(D * W + j * D, D), :].astype(jnp.bfloat16)
+    small_ref[...] = flat[pl.ds(MATRIX_ROWS, SMALL_ROWS), :]
+    cots.finish()
+    for h in range(1, far):
+        remote(attn_ref, held.at[mine, at.hi], send_z.at[h], recv_z.at[h], beyond[h - 1]).wait_send()
+
+
+def rows_kernel(ctx, own_ref, out_ref, *sems):
+    at = Place(ctx)
+    greet(at.cube())
+    gather = CubeGather(at, own_ref, out_ref, sems)
+    gather.push()
+    out_ref[at.slot((at.lo, at.c))] = own_ref[...]
+    gather.forward()
+    gather.finish()
+
+
+def sum_kernel(ctx, part_ref, out_ref, buf1, tmp, buf2, *sems):
+    at = Place(ctx)
+    greet(at.cube())
+    scatter = CubeScatter(at, part_ref, (buf1, tmp, buf2), sems)
+    scatter.push()
+    scatter.forward()
+    out_ref[...] = scatter.finish()
+    scatter.drain()
+
+
+def stream_sum_kernel(ctx, part_ref, out_ref, buf, send, recv):
+    hi, lo, c = lax.axis_index("hi"), lax.axis_index("lo"), lax.axis_index("ctx")
+    others = [lax.rem(c + d, ctx) for d in range(1, ctx)]
+    greet([(hi, lo, other) for other in others])
+    copies = []
+    for d, other in enumerate(others):
+        copy = remote(part_ref.at[other], buf.at[d], send.at[d], recv.at[d], (hi, lo, other))
+        copy.start()
+        copies.append(copy)
+    total = part_ref[c].astype(jnp.float32)
+    for d, copy in enumerate(copies):
+        copy.wait()
+        total = total + buf[d].astype(jnp.float32)
+    out_ref[...] = total
+
+
+def grads_kernel(far, ctx, shard, pad, *refs):
+    qkv_ref, gout_ref, small_ref, part_ref, attn_ref, sum_ref = refs[:6]
+    flat, held, col, low, buf3 = refs[6:11]
+    attn_bufs, sum_bufs = refs[11:14], refs[14:17]
+    send_z, recv_z = refs[17:19]
+    attn_sems, sum_sems = refs[19:23], refs[23:27]
+    at = Place(ctx)
+    beyond = [(lax.rem(at.hi + h, far), at.lo, at.c) for h in range(1, far)]
+    greet(at.cube() + beyond)
+    sums = CubeScatter(at, part_ref, sum_bufs, sum_sems)
+    sums.push()
+    for j in range(W):
+        cols = pl.ds(j * LANES, LANES)
+        flat[pl.ds(j, D, stride=W), :] = qkv_ref[:, cols]
+        flat[pl.ds(D * W + 2 * D + j, D, stride=W), :] = gout_ref[:, cols]
+    for j in range(2):
+        flat[pl.ds(D * W + j * D, D), :] = qkv_ref[:, pl.ds(D + j * LANES, LANES)]
+    flat[pl.ds(MATRIX_ROWS, SMALL_ROWS), :] = small_ref[...]
+    tail = MATRIX_ROWS + SMALL_ROWS
+    flat[pl.ds(tail, flat.shape[0] - tail), :] = jnp.zeros((flat.shape[0] - tail, LANES), jnp.float32)
+    for g in range(far * 2 * ctx):
+        block = flat[pl.ds(g * shard, pad), :]
+        held[g % (2 * ctx), g // (2 * ctx)] = block.astype(jnp.bfloat16)
+    grads = CubeScatter(at, held, attn_bufs, attn_sems)
+    grads.push()
+    grads.forward()
+    sums.forward()
+    col[...] = grads.finish()
+    low[...] = col[...].astype(jnp.bfloat16)
+    crossing = []
+    for h in range(1, far):
+        copy = remote(low.at[beyond[h - 1][0]], buf3.at[h], send_z.at[h], recv_z.at[h], beyond[h - 1])
+        copy.start()
+        crossing.append(copy)
+    sum_ref[...] = sums.finish()
+    total = col[at.hi]
+    for h in range(1, far):
+        crossing[h - 1].wait()
+        total = total + buf3[h].astype(jnp.float32)
+    attn_ref[...] = total
+    grads.drain()
+    sums.drain()
+
+
+def call(kernel, outs, scratch, number, *args):
+    vmem = pl.BlockSpec(memory_space=pltpu.VMEM)
+    return pl.pallas_call(
+        kernel,
+        out_shape=[jax.ShapeDtypeStruct(shape, kind) for shape, kind in outs],
+        in_specs=[vmem] * len(args),
+        out_specs=[vmem] * len(outs),
+        scratch_shapes=scratch,
+        compiler_params=pltpu.CompilerParams(
+            collective_id=number, has_side_effects=True, vmem_limit_bytes=48 * 2**20
+        ),
+    )(*args)
+
+
+def dma(*shape):
+    return pltpu.SemaphoreType.DMA(shape)
+
+
+def padded(shard):
+    return -(-shard // 16) * 16
+
+
+def gather_params(attn_rows, cot_low, far, ctx):
+    shard = attn_rows.shape[0]
+    pad = padded(shard)
+    cube, n = 2 * ctx, ctx
+    total = shard * far * cube + pad - shard
+    attn_rows = jnp.pad(attn_rows, ((0, pad - shard), (0, 0)))
+    bf16 = jnp.bfloat16
+    outs = [
+        ((D, QKV), bf16),
+        ((D, D), bf16),
+        ((SMALL_ROWS, LANES), jnp.float32),
+        ((cube,) + cot_low.shape, bf16),
     ]
-    pieces = []
-    offset = 0
-    for piece_shape in shapes_list:
-        entries = math.prod(piece_shape)
-        pieces.append(flat_params[offset : offset + entries].reshape(piece_shape))
-        offset += entries
-    return pieces
-
-
-def pack_grads(pieces, total_length):
-    flat_grad = jnp.concatenate([piece.reshape(-1) for piece in pieces])
-    padding = total_length - flat_grad.shape[0]
-    return jnp.concatenate([flat_grad, jnp.zeros((padding,), jnp.float32)])
+    scratch = [
+        pltpu.VMEM((cube, far, pad, LANES), bf16),
+        pltpu.VMEM((total, LANES), jnp.float32),
+        dma(far),
+        dma(far),
+    ]
+    scratch += [dma(far, n)] * 4 + [dma(n)] * 4
+    kernel = functools.partial(params_kernel, far, ctx, shard, pad)
+    return call(kernel, outs, scratch, 0, attn_rows, cot_low)
+
+
+def gather_rows(rows_low, ctx):
+    outs = [((2 * ctx,) + rows_low.shape, jnp.bfloat16)]
+    return call(functools.partial(rows_kernel, ctx), outs, [dma(ctx)] * 4, 1, rows_low)[0]
+
+
+def sum_rows(part, ctx):
+    block = part.shape[1:]
+    scratch = [pltpu.VMEM((ctx,) + block, jnp.bfloat16)] * 3 + [dma(ctx)] * 4
+    return call(functools.partial(sum_kernel, ctx), [(block, jnp.float32)], scratch, 2, part)[0]
+
+
+def stream_sum(part, ctx):
+    block = part.shape[1:]
+    scratch = [pltpu.VMEM((ctx - 1,) + block, jnp.bfloat16), dma(ctx - 1), dma(ctx - 1)]
+    return call(functools.partial(stream_sum_kernel, ctx), [(block, jnp.float32)], scratch, 3, part)[0]
+
+
+def scatter_grads(grad_qkv, grad_out, small, part, shard, far, ctx):
+    pad = padded(shard)
+    cube, n = 2 * ctx, ctx
+    total = shard * far * cube + pad - shard
+    block = part.shape[1:]
+    bf16 = jnp.bfloat16
+    column = (far, pad, LANES)
+    scratch = [
+        pltpu.VMEM((total, LANES), jnp.float32),
+        pltpu.VMEM((cube,) + column, bf16),
+        pltpu.VMEM(column, jnp.float32),
+        pltpu.VMEM(column, bf16),
+        pltpu.VMEM(column, bf16),
+    ]
+    scratch += [pltpu.VMEM((n,) + column, bf16)] * 3 + [pltpu.VMEM((n,) + block, bf16)] * 3
+    scratch += [dma(far)] * 2 + [dma(n)] * 8
+    kernel = functools.partial(grads_kernel, far, ctx, shard, pad)
+    outs = [((pad, LANES), jnp.float32), (block, jnp.float32)]
+    attn, out_sum = call(kernel, outs, scratch, 4, grad_qkv, grad_out, small, part)
+    return attn[:shard], out_sum
 
 
 def per_device(tokens, seq_lengths, attn_params, ffn_weight, out_grad):
@@ -96,19 +409,17 @@
     score_scale = HEAD ** (-0.5)
     units = ffn_weight.shape[1]
     far = lax.axis_size("hi")
-    devices = far * lax.axis_size("lo") * lax.axis_size("ctx")
-    total_length = attn_params.shape[0] * devices
+    ctx = lax.axis_size("ctx")
+    cube = 2 * ctx
     f32, bf16 = jnp.float32, jnp.bfloat16
 
     cot_low = out_grad.reshape(rows, D)
     ffn_all = lax.all_gather(ffn_weight.reshape(3 * units, D), "hi", axis=0, tiled=False)
-    attn_all = lax.all_gather(
-        attn_params.reshape(-1, 128), ("hi", "lo", "ctx"), axis=0, tiled=False
-    ).reshape(-1)
-    cot_all = lax.all_gather(cot_low, ("lo", "ctx"), axis=0, tiled=True)
-    w_query, w_key, w_value, w_out, b_query, b_key, b_value, gain_one, gain_two = unpack(attn_all)
-    w_qkv = jnp.concatenate([w_query, w_key, w_value], axis=1)
-    b_qkv = jnp.concatenate([b_query, b_key, b_value], axis=0).astype(f32)
+    attn_rows = attn_params.reshape(-1, LANES)
+    w_qkv, w_out, small, cot_all = gather_params(attn_rows, cot_low, far, ctx)
+    cot_all = cot_all.reshape(-1, D)
+    small = small.reshape(-1)
+    b_qkv, gain_one, gain_two = small[:QKV], small[QKV : QKV + D], small[QKV + D : QKV + 2 * D]
 
     slot_ids = jnp.arange(stream, dtype=jnp.int32)
     first_slot = lax.axis_index("ctx") * rows_own
@@ -123,7 +434,7 @@
     )
 
     x_float = tokens.reshape(rows, D).astype(f32)
-    normed, norm_pull = jax.vjp(rms_norm, x_float, gain_one.astype(f32))
+    normed, norm_pull = jax.vjp(rms_norm, x_float, gain_one)
     normed_low = normed.astype(bf16)
     qkv = jnp.dot(normed_low, w_qkv, preferred_element_type=f32) + b_qkv
     query_pre, key_pre, value_pre = jnp.split(qkv, [D, D + kv_width], axis=1)
@@ -146,10 +457,10 @@
     mixed = jnp.einsum("mkgqs,mskd->mqkgd", probs_low, values_all, preferred_element_type=f32)
     mixed_low = mixed.reshape(rows, HEADS * HEAD).astype(bf16)
     second = x_float + jnp.dot(mixed_low, w_out, preferred_element_type=f32)
-    normed_two, norm_two_pull = jax.vjp(rms_norm, second, gain_two.astype(f32))
+    normed_two, norm_two_pull = jax.vjp(rms_norm, second, gain_two)
     two_low = normed_two.astype(bf16)
 
-    two_all = lax.all_gather(two_low, ("lo", "ctx"), axis=0, tiled=True)
+    two_all = gather_rows(two_low, ctx).reshape(-1, D)
     ffn_all = ffn_all.reshape(far, 3, units, D).transpose(1, 0, 2, 3).reshape(3, far * units, D)
     w_gate, w_up, w_down = ffn_all[0], ffn_all[1], ffn_all[2]
     d_hidden = jnp.einsum("td,fd->tf", cot_all, w_down, preferred_element_type=f32)
@@ -162,19 +473,15 @@
     up_low = (d_hidden * silu).astype(bf16)
     d_two_part = jnp.einsum("tf,fd->td", gate_low, w_gate, preferred_element_type=f32)
     d_two_part += jnp.einsum("tf,fd->td", up_low, w_up, preferred_element_type=f32)
-    d_two = lax.psum_scatter(
-        d_two_part.astype(bf16), ("lo", "ctx"), scatter_dimension=0, tiled=True
-    ).astype(f32)
+    d_two = sum_rows(d_two_part.astype(bf16).reshape(cube, rows, D), ctx)
     out_part = jnp.einsum("tf,fd->td", hidden_low, w_down, preferred_element_type=f32)
-    out_sum = lax.psum_scatter(
-        out_part.astype(bf16), ("lo", "ctx"), scatter_dimension=0, tiled=True
-    ).astype(f32)
-    result = (second + out_sum).astype(bf16)
     grad_gate = jnp.einsum("tf,td->fd", gate_low, two_all, preferred_element_type=f32)
     grad_up = jnp.einsum("tf,td->fd", up_low, two_all, preferred_element_type=f32)
     grad_down = jnp.einsum("tf,td->fd", hidden_low, cot_all, preferred_element_type=f32)
-    ffn_part = jnp.stack([grad_gate, grad_up, grad_down], axis=0).astype(bf16)
-    ffn_grad = lax.psum_scatter(ffn_part, "hi", scatter_dimension=1, tiled=True).astype(f32)
+    ffn_part = jnp.stack([grad_gate.astype(bf16), grad_up.astype(bf16), grad_down.astype(bf16)])
+    ffn_part = ffn_part.reshape(3, far, units, D).transpose(1, 0, 2, 3).reshape(far, 3 * units, D)
+    ffn_grad = lax.psum_scatter(ffn_part, "hi", scatter_dimension=0, tiled=False)
+    ffn_grad = ffn_grad.astype(f32).reshape(3, units, D)
 
     d_second_part, d_gain_two = norm_two_pull(d_two)
     d_second = cot_low.astype(f32) + d_second_part
@@ -200,38 +507,34 @@
         ],
         axis=2,
     )
-    dkv = lax.psum_scatter(dkv_part.astype(bf16), "ctx", scatter_dimension=1, tiled=True)
-    dkv = dkv.reshape(rows, 2 * kv_width)
+    dkv_part = dkv_part.astype(bf16).reshape(micro_count, ctx, rows_own, 2 * kv_width)
+    dkv = stream_sum(dkv_part.transpose(1, 0, 2, 3).reshape(ctx, rows, 2 * kv_width), ctx)
     dq_low = (
         rotate_back(dq_rot.reshape(rows, HEADS, HEAD), cos_heads, sin_heads)
         .reshape(rows, HEADS * HEAD)
         .astype(bf16)
     )
-    dk_rot = dkv[:, :kv_width].astype(f32).reshape(rows, KV_HEADS, HEAD)
+    dk_rot = dkv[:, :kv_width].reshape(rows, KV_HEADS, HEAD)
     dk_low = rotate_back(dk_rot, cos_heads, sin_heads).reshape(rows, kv_width).astype(bf16)
-    d_qkv = jnp.concatenate([dq_low, dk_low, dkv[:, kv_width:]], axis=1)
+    d_qkv = jnp.concatenate([dq_low, dk_low, dkv[:, kv_width:].astype(bf16)], axis=1)
     d_normed = jnp.einsum("te,de->td", d_qkv, w_qkv, preferred_element_type=f32)
     d_input_part, d_gain_one = norm_pull(d_normed)
     input_grad = (d_second + d_input_part).astype(bf16)
     grad_qkv = jnp.einsum("td,te->de", normed_low, d_qkv, preferred_element_type=f32)
     grad_out = jnp.einsum("td,te->de", mixed_low, branch_low, preferred_element_type=f32)
     grad_bias = jnp.sum(d_qkv.astype(f32), axis=0)
-    pieces = [
-        grad_qkv[:, :D],
-        grad_qkv[:, D : D + kv_width],
-        grad_qkv[:, D + kv_width :],
+    zeros = jnp.zeros((SMALL_ROWS * LANES - QKV - 2 * D,), f32)
+    small_grad = jnp.concatenate([grad_bias, d_gain_one, d_gain_two, zeros])
+    attn_grad, out_sum = scatter_grads(
+        grad_qkv,
         grad_out,
-        grad_bias,
-        d_gain_one,
-        d_gain_two,
-    ]
-    flat_grad = pack_grads(pieces, total_length)
-    attn_grad = lax.psum_scatter(
-        flat_grad.astype(bf16).reshape(devices, -1, 128),
-        ("hi", "lo", "ctx"),
-        scatter_dimension=0,
-        tiled=True,
-    ).astype(f32)
+        small_grad.reshape(SMALL_ROWS, LANES),
+        out_part.astype(bf16).reshape(cube, rows, D),
+        attn_rows.shape[0],
+        far,
+        ctx,
+    )
+    result = (second + out_sum).astype(bf16)
     shape = tokens.shape
     return (result.reshape(shape), input_grad.reshape(shape), attn_grad.reshape(-1), ffn_grad)
 

time: 562 us -> 221 us (0.39)
  waiting for transfers between devices: 399 us -> 0.72 us
  Pallas kernels: 0 us -> 119 us
  local copies, waits for them, and re-layouts: 62.4 us -> 24.4 us
  matrix products: 49.7 us -> 38.4 us
  other arithmetic: 26.7 us -> 16.7 us
    unnamed x11 -> x3, waiting for transfers between devices: 202 us -> 0.7 us
    pallas_call x0 -> x5, Pallas kernels: none -> 119 us  [call(): pl.pallas_call(kernel, out_shape=[jax.ShapeDtypeStruct(shape, kind) for s...]
    all_gather x3 -> x0, waiting for transfers between devices: 104 us -> none  [the longest x1 58.4 us: per_device(): lax.all_gather(attn_params.reshape(-1, 128), ('hi', 'lo', 'ctx'), axis=0,...]
    reduce_scatter x3 -> x0, waiting for transfers between devices: 75.2 us -> none  [the longest x1 41.8 us: per_device(): lax.psum_scatter(out_part.astype(bf16), ('lo', 'ctx'), scatter_dimension=...]
    all_gather x1, waiting for transfers between devices: 17.8 us -> 0.02 us  [per_device(): lax.all_gather(ffn_weight.reshape(3 * units, D), 'hi', axis=0, tiled=False)]
    reshape x7 -> x1, local copies, waits for them, and re-layouts: 16.2 us -> 0.7 us  [per_device(): attn_grad.reshape(-1)]
    slice x5 -> x4, local copies, waits for them, and re-layouts: 10.4 us -> 0.22 us  [the longest x2 0.13 us: per_device(): dkv[:, kv_width:].astype(bf16)]
    unnamed x76 -> x80, local copies, waits for them, and re-layouts: 13.5 us -> 8.87 us
  transfers between devices with their start and end apart: 9 -> 2, of which waited for: 9 -> 0; matrix products, arithmetic and copies ran while one was open for 20% -> 23% of each run, Pallas kernels for 0% -> 54%
where the time goes in v2:
time: 221 us; the launch traced here: 220 us
  Pallas kernels  119 us (54%)
  matrix products  38.4 us (17%)
  local copies, waits for them, and re-layouts  24.4 us (11%)
  other arithmetic  16.7 us (8%)
  between operations  15 us (7%)
  blocking collectives  6.02 us (3%)
    pallas_call x5, Pallas kernels, call(): pl.pallas_call(kernel, out_shape=[jax.ShapeDtypeStruct(shape, kind) for s...  119 us
    unnamed x80, local copies, waits for them, and re-layouts  8.87 us
    all_gather x1, blocking collectives, per_device(): lax.all_gather(kv_low.reshape(micro_count, rows_own, 2 * kv_width), 'ctx'...  6.02 us
  transfers between devices with their start and end apart: 2, of which 0 were waited for; matrix products, arithmetic and copies ran while one was open for 23% of the time, Pallas kernels for 54%

profile of v2, /device:TPU:0, one launch (start us, length us, event | category | flops | bytes accessed | tf_op | source)
XLA Modules:
  0.0 219.8 jit_solution(7567795854854041326)
XLA Ops:
  11.6 40.1 %shard_map.84 = (bf16[896,1152]{1,0:T(8,128)(2,1)S(1)}, bf16[896,896]{1,0:T(8,128)(2,1)S(1)}, f32[24,128]{1,0:T(8,128)S(1)}, bf16[8,128,896]{2,1,0:T(8,128)(2,1)S(1)}) custom-call(bf16[464,128]{1,0:T(8,128)(2,1)S(1)} %pad.4.refs_0_, bf16[128,896]{1,0:T(8,128)(2,1)S(1)} %bitcast.203), custom_call_target="tpu_custom_call" | custom-call | tf_op jit(solution)/shard_map/pallas_call | solution.py:320
  56.1 2.1 convolution_add_fusion
  60.6 6.0 %all_gather.6 = bf16[2,256,256]{2,0,1:T(2,128)(2,1)S(1)} all-gather(bf16[2,64,256]{2,0,1:T(2,128)(2,1)S(1)} %pad_maximum_fusion.3), channel_id=1, replica_groups=mesh['hi'=4,'lo'=2,'ctx'=4] {'ctx'}, dimensions={1}, use_global_device_ids=true | all-gather | bytes 327680 | tf_op jit(solution)/shard_map/all_gather | solution.py:444
  74.6 2.6 %fusion.14 = bf16[2,64,2,7,64]{1,0,4,3,2:T(2,128)(2,1)} fusion(f32[2,64,2,7,32]{1,0,4,3,2:T(2,128)} %concatenate.65, f32[2,64,2,7,32]{1,0,4,3,2:T(2,128)S(1)} %concatenate.64, f32[2,64,2,7,64]{1,0,4,3,2:T(2,128)S(1)} %reshape.305, f32[2,64,64]{1,0,2:T(2,128)S(1)} %get-tuple-element.50, f32[2,64,64]{1,0,2:T(2,128)S(1)} %get-tuple-element.49), kind=kLoop, calls=%fused_computation.36 | loop fusion | flops 573440 | bytes 1212416 | tf_op jit(solution)/shard_map/convert_element_type | solution.py:441
  77.1 3.0 %fusion.54 = (f32[2,2,7,64]{3,2,1,0:T(8,128)S(1)}, f32[2,2,7,64,256]{4,3,2,1,0:T(8,128)}) fusion(pred[2,64,256]{2,1,0:T(8,128)(4,1)S(1)} %compare_and_fusion, bf16[2,64,2,7,64]{1,0,4,3,2:T(2,128)(2,1)} %fusion.14, bf16[2,256,2,2,64]{1,4,3,2,0:T(8,128)(2,1)} %bitcast.221), kind=kOutput, calls=%fused_computation.134 | convolution fusion | flops 60555520 | bytes 2464768 | tf_op jit(solution)/shard_map/sub | solution.py:455
  80.2 2.1 fusion.7
  84.5 15.0 %shard_map.85 = bf16[8,128,896]{2,1,0:T(8,128)(2,1)S(1)} custom-call(bf16[128,896]{1,0:T(8,128)(2,1)S(1)} %multiply_convert_fusion.3.own_ref), custom_call_target="tpu_custom_call" | custom-call | tf_op jit(solution)/shard_map/pallas_call | solution.py:320
  99.4 2.2 fusion.51
  101.7 1.5 fusion.58
  103.9 1.5 fusion.57
  105.4 2.4 %multiply_convert_fusion = (bf16[1024,608]{0,1:T(8,128)(2,1)S(1)}, bf16[1024,608]{0,1:T(8,128)(2,1)S(1)}, bf16[1024,608]{0,1:T(8,128)(2,1)S(1)}) fusion(f32[1024,608]{0,1:T(8,128)S(1)} %fusion.58, f32[1024,608]{0,1:T(8,128)S(1)} %fusion.57, bf16[1024,896]{1,0:T(8,128)(2,1)S(1)} %bitcast.198, bf16[608,896]{1,0:T(8,128)(2,1)S(1)} %bitcast.212), kind=kOutput, calls=%fused_computation.4 | convolution fusion | flops 1125023744 | bytes 11640832 | tf_op jit(solution)/shard_map/td,fd->tf/dot_general | solution.py:468
  109.3 3.8 %fusion.59 = f32[1024,896]{1,0:T(8,128)} fusion(bf16[1024,608]{0,1:T(8,128)(2,1)S(1)} %get-tuple-element.21, bf16[608,896]{1,0:T(8,128)(2,1)S(1)} %bitcast.215), kind=kOutput, calls=%fused_computation.137 | convolution fusion | flops 1115684864 | bytes 6004736 | tf_op jit(solution)/shard_map/tf,fd->td/dot_general | solution.py:474
  113.1 1.5 convolution_convert_fusion.2
  114.6 1.5 convolution_convert_fusion.1
  116.1 2.1 pad_maximum_fusion
  119.5 4.2 %add_convert_fusion = bf16[1024,896]{1,0:T(8,128)(2,1)S(1)} fusion(f32[1024,896]{1,0:T(8,128)} %fusion.59, bf16[1024,608]{0,1:T(8,128)(2,1)} %copy-done.37, bf16[608,896]{1,0:T(8,128)(2,1)S(1)} %bitcast.213), kind=kOutput, calls=%fused_computation.1 | convolution fusion | flops 1117519872 | bytes 7839744 | tf_op jit(solution)/shard_map/tf,fd->td/dot_general | solution.py:475
  123.7 15.5 %shard_map.86 = f32[128,896]{1,0:T(8,128)S(1)} custom-call(bf16[8,128,896]{2,1,0:T(8,128)(2,1)S(1)} %bitcast.201), custom_call_target="tpu_custom_call" | custom-call | tf_op jit(solution)/shard_map/pallas_call | solution.py:320
  141.0 2.4 %fusion.2 = (f32[2,2,7,64]{3,2,1,0:T(8,128)S(1)}, f32[2,2,256,64,7]{2,3,4,1,0:T(8,128)S(1)}) fusion(f32[2,2,7,64,256]{4,3,2,1,0:T(8,128)} %get-tuple-element.41, f32[2,2,7,64]{3,2,1,0:T(8,128)S(1)} %copy-done.27, bf16[2,64,2,7,64]{1,4,3,2,0:T(8,128)(2,1)S(1)} %copy.92, bf16[2,256,2,2,64]{1,4,3,2,0:T(8,128)(2,1)S(1)} %bitcast.223), kind=kOutput, calls=%fused_computation.11 | convolution fusion | flops 60094720 | bytes 4283392 | tf_op jit(solution)/shard_map/mqkgd,mskd->mkgqs/dot_general | solution.py:491
  149.3 2.0 fusion.12
  151.7 5.0 %shard_map.87 = f32[128,256]{1,0:T(8,128)S(1)} custom-call(bf16[4,128,256]{2,1,0:T(8,128)(2,1)S(1)} %bitcast.202), custom_call_target="tpu_custom_call" | custom-call | tf_op jit(solution)/shard_map/pallas_call | solution.py:320
  160.7 2.7 %fusion.50.refs_0_ = f32[896,1152]{1,0:T(8,128)} fusion(bf16[128,896]{1,0:T(8,128)(2,1)S(1)} %copy-done.11, bf16[128,128]{0,1:T(8,128)(2,1)S(1)} %copy.99, bf16[128,128]{0,1:T(8,128)(2,1)S(1)} %copy.98, bf16[128,896]{0,1:T(8,128)(2,1)S(1)} %fusion.21), kind=kOutput, calls=%fused_computation.130 | convolution fusion | flops 265125888 | bytes 4653056 | tf_op jit(solution)/shard_map/td,te->de/dot_general | solution.py:523
  163.4 1.8 convolution_convert_fusion
  165.2 43.0 %shard_map.88 = (f32[464,128]{1,0:T(8,128)S(1)}, f32[128,896]{1,0:T(8,128)S(1)}) custom-call(f32[896,1152]{1,0:T(8,128)} %fusion.50.refs_0_, f32[896,896]{1,0:T(8,128)S(1)} %fusion.38.refs_1_, f32[24,128]{1,0:T(8,128)S(1)} %maximum_bitcast_fusion.1.refs_2_, bf16[8,128,896]{2,1,0:T(8,128)(2,1)S(1)} %bitcast.196), custom_call_target="tpu_custom_call" | custom-call | tf_op jit(solution)/shard_map/pallas_call | solution.py:320
  210.6 2.4 %convert.22 = f32[3,152,896]{2,1,0:T(8,128)} convert(bf16[3,152,896]{2,1,0:T(8,128)(2,1)} %bitcast.220) | non-fusion elementwise | flops 408576 | bytes 2451456 | tf_op jit(solution)/shard_map/convert_element_type | solution.py:484
  (181 shorter events, 38.6 us)
Async XLA Ops:
  7.2 48.4 %copy-start.8 = (bf16[2,64,896]{2,1,0:T(8,128)(2,1)S(1)}, bf16[2,64,896]{2,1,0:T(8,128)(2,1)}, u32[]{:S(2)}) copy-start(bf16[2,64,896]{2,1,0:T(8,128)(2,1)} %param.5) | copy-start | bytes 688132
  7.2 92.3 %all-gather.2.cloned.1.call-start = ((), (), s32[]{:S(2)}) async-start(), calls=%async_computation.1 | async-start | bytes 4085760 | tf_op jit(solution)/shard_map/all_gather | solution.py:417
  7.9 202.7 %reduce-scatter.4.cloned.1.call-start = ((), (), s32[]{:S(2)}) async-start(), calls=%async_computation.2 | async-start | bytes 4085760
  9.8 49.5 %copy-start.32 = (s32[2]{0:T(128)}, s32[2]{0:T(128)S(1)}, u32[]{:S(2)}) copy-start(s32[2]{0:T(128)S(1)} %slice_reduce_fusion) | copy-start | bytes 28
  55.7 3.3 %copy-start.10 = (bf16[128,896]{1,0:T(8,128)(2,1)}, bf16[128,896]{1,0:T(8,128)(2,1)S(1)}, u32[]{:S(2)}) copy-start(bf16[128,896]{1,0:T(8,128)(2,1)S(1)} %fusion.25) | copy-start | bytes 688132
  60.2 7.3 %copy-start.24 = (f32[128,64]{0,1:T(8,128)}, f32[128,64]{0,1:T(8,128)S(1)}, u32[]{:S(2)}) copy-start(f32[128,64]{0,1:T(8,128)S(1)} %get-tuple-element.47) | copy-start | bytes 98308
  77.1 3.0 %copy-start.20 = (bf16[2,256,256]{1,2,0:T(8,128)(2,1)S(1)}, bf16[2,256,256]{1,2,0:T(8,128)(2,1)}, u32[]{:S(2)}) copy-start(bf16[2,256,256]{1,2,0:T(8,128)(2,1)} %copy.79) | copy-start | bytes 786436
  80.2 2.1 copy-start.26
  83.6 18.1 %copy-start.33 = (f32[128]{0:T(128)}, f32[128]{0:T(128)S(1)}, u32[]{:S(2)}) copy-start(f32[128]{0:T(128)S(1)} %get-tuple-element.42) | copy-start | bytes 1540
  101.6 3.8 %copy-start.18 = (bf16[1,4,152,896]{3,2,0,1:T(8,128)(2,1)}, bf16[1,4,152,896]{3,2,0,1:T(8,128)(2,1)S(1)}, u32[]{:S(2)}) copy-start(bf16[1,4,152,896]{3,2,0,1:T(8,128)(2,1)S(1)} %get-tuple-element.23) | copy-start | bytes 3268612
  101.6 2.3 %copy-start.5 = (bf16[8,128,896]{2,1,0:T(8,128)(2,1)S(1)}, bf16[8,128,896]{2,1,0:T(8,128)(2,1)}, u32[]{:S(2)}) copy-start(bf16[8,128,896]{2,1,0:T(8,128)(2,1)} %copy-done.4) | copy-start | bytes 5505028
  107.8 5.3 %copy-start.37 = (bf16[1024,608]{0,1:T(8,128)(2,1)}, bf16[1024,608]{0,1:T(8,128)(2,1)S(1)}, u32[]{:S(2)}) copy-start(bf16[1024,608]{0,1:T(8,128)(2,1)S(1)} %get-tuple-element.22) | copy-start | bytes 3735556
  107.8 6.8 %copy-start.38 = (bf16[1024,608]{0,1:T(8,128)(2,1)}, bf16[1024,608]{0,1:T(8,128)(2,1)S(1)}, u32[]{:S(2)}) copy-start(bf16[1024,608]{0,1:T(8,128)(2,1)S(1)} %get-tuple-element.20) | copy-start | bytes 3735556
  123.7 15.5 %copy-start.7 = (f32[128,896]{1,0:T(8,128)S(1)}, f32[128,896]{1,0:T(8,128)}, u32[]{:S(2)}) copy-start(f32[128,896]{1,0:T(8,128)} %copy-done.6) | copy-start | bytes 1376260
  123.7 15.7 %copy-start.34 = (f32[128]{0:T(128)S(1)}, f32[128]{0:T(128)}, u32[]{:S(2)}) copy-start(f32[128]{0:T(128)} %copy-done.33) | copy-start | bytes 1540
  123.7 15.7 %copy-start.3 = (bf16[2,64,896]{2,1,0:T(8,128)(2,1)S(1)}, bf16[2,64,896]{2,1,0:T(8,128)(2,1)}, u32[]{:S(2)}) copy-start(bf16[2,64,896]{2,1,0:T(8,128)(2,1)} %param.9) | copy-start | bytes 688132
  141.0 2.5 %copy-start.22 = (bf16[2,64,2,7,64]{1,4,3,2,0:T(8,128)(2,1)}, bf16[2,64,2,7,64]{1,4,3,2,0:T(8,128)(2,1)S(1)}, u32[]{:S(2)}) copy-start(bf16[2,64,2,7,64]{1,4,3,2,0:T(8,128)(2,1)S(1)} %copy.92) | copy-start | bytes 688132
  141.0 2.5 %copy-start.14 = (f32[2,2,7,64,256]{4,3,2,1,0:T(8,128)S(1)}, f32[2,2,7,64,256]{4,3,2,1,0:T(8,128)}, u32[]{:S(2)}) copy-start(f32[2,2,7,64,256]{4,3,2,1,0:T(8,128)} %get-tuple-element.41) | copy-start | bytes 5505028
  147.0 2.3 %copy-start.28 = (f32[2,2,7,64]{3,2,1,0:T(8,128)S(1)}, f32[2,2,7,64]{3,2,1,0:T(8,128)}, u32[]{:S(2)}) copy-start(f32[2,2,7,64]{3,2,1,0:T(8,128)} %copy-done.26) | copy-start | bytes 21508
  151.3 6.0 %copy-start.15 = (f32[128,14,64]{0,2,1:T(8,128)S(1)}, f32[128,14,64]{0,2,1:T(8,128)}, u32[]{:S(2)}) copy-start(f32[128,14,64]{0,2,1:T(8,128)} %reshape.313) | copy-start | bytes 1376260
  157.6 2.2 copy-start.13
  160.7 2.7 %copy-start.17 = (bf16[1,4,152,896]{3,2,0,1:T(8,128)(2,1)S(1)}, bf16[1,4,152,896]{3,2,0,1:T(8,128)(2,1)}, u32[]{:S(2)}) copy-start(bf16[1,4,152,896]{3,2,0,1:T(8,128)(2,1)} %copy-done.16) | copy-start | bytes 3268612
  160.7 2.7 %copy-start.39 = (bf16[1024,608]{0,1:T(8,128)(2,1)S(1)}, bf16[1024,608]{0,1:T(8,128)(2,1)}, u32[]{:S(2)}) copy-start(bf16[1024,608]{0,1:T(8,128)(2,1)} %copy-done.38) | copy-start | bytes 3735556
  165.2 43.0 %copy-start.36 = (f32[128]{0:T(128)S(1)}, f32[128]{0:T(128)}, u32[]{:S(2)}) copy-start(f32[128]{0:T(128)} %copy-done.35) | copy-start | bytes 1540
  (18 other events, 20.5 us)
Sparse Core Ops, SparseCore 0:
  9.6 72.3 all-gather.1
  118.4 62.4 reduce-scatter.3

commit v3 on v2

--- a/solution.py
+++ b/solution.py
@@ -67,6 +67,8 @@
 MATRIX_ROWS = 2 * D * W + 2 * D * KV_HEADS * HEAD // LANES
 SMALL_ROWS = 24
 MESH = pl.DeviceIdType.MESH
+NEAR = [(0, 0), (0, 1), (1, 0), (1, 1)]
+N = len(NEAR)
 
 
 class Place:
@@ -76,27 +78,24 @@
         self.lo = lax.axis_index("lo")
         self.c = lax.axis_index("ctx")
         self.sib = self.c + 1 - 2 * lax.rem(self.c, 2)
-        self.rels = [(a, b) for a in range(2) for b in range(ctx // 2)]
-        self.n = len(self.rels)
-
-    def to(self, r, c=None):
-        a, b = self.rels[r]
+
+    def of(self, r, c=None):
         c = self.c if c is None else c
+        a, b = NEAR[r]
         return lax.rem(self.lo + a, 2), lax.rem(c + 2 * b, self.ctx)
 
-    def source(self, r, c=None):
-        a, b = self.rels[r]
-        c = self.c if c is None else c
-        return lax.rem(self.lo + 2 - a, 2), lax.rem(c + self.ctx - 2 * b, self.ctx)
-
-    def slot(self, pair):
-        return pair[0] * self.ctx + pair[1]
-
-    def cube(self):
-        return [(self.hi,) + self.to(r) for r in range(1, self.n)] + [self.sibling()]
+    def slot(self, r, c=None):
+        lo, c = self.of(r, c)
+        return lo * self.ctx + c
+
+    def device(self, r):
+        return (self.hi,) + self.of(r)
 
     def sibling(self):
         return (self.hi, self.lo, self.sib)
+
+    def cube(self):
+        return [self.device(1), self.device(2), self.sibling()]
 
 
 def greet(devices):
@@ -113,79 +112,119 @@
     )
 
 
-class CubeGather:
-    def __init__(self, at, own, out, sems, aim=lambda out, slot: out.at[slot]):
-        self.at, self.own, self.out, self.aim = at, own, out, aim
+class Unit:
+    def __init__(self, at, turn, sems):
+        self.at = at
+        self.first, self.second = (1, 2) if turn % 2 == 0 else (2, 1)
         self.send1, self.recv1, self.send2, self.recv2 = sems
         self.started = []
 
-    def go(self, copy):
+    def go(self, *parts):
+        copy = remote(*parts)
         copy.start()
         self.started.append(copy)
-
-    def push(self):
-        at = self.at
-        mine = self.aim(self.out, at.slot((at.lo, at.c)))
-        for r in range(1, at.n):
-            self.go(remote(self.own, mine, self.send1.at[r], self.recv1.at[r], (at.hi,) + at.to(r)))
-        self.go(remote(self.own, mine, self.send2.at[0], self.recv2.at[0], at.sibling()))
-
-    def forward(self):
-        at = self.at
-        for r in range(1, at.n):
-            here = self.aim(self.out, at.slot(at.source(r)))
-            remote(here, here, self.send1.at[r], self.recv1.at[r], (at.hi,) + at.to(r)).wait_recv()
-            self.go(remote(here, here, self.send2.at[r], self.recv2.at[r], at.sibling()))
-
-    def finish(self):
-        at = self.at
-        for r in range(at.n):
-            here = self.aim(self.out, at.slot(at.source(r, at.sib)))
-            remote(here, here, self.send2.at[r], self.recv2.at[r], at.sibling()).wait_recv()
-        for copy in self.started:
-            copy.wait_send()
-
-
-class CubeScatter:
-    def __init__(self, at, part, bufs, sems):
-        self.at, self.part = at, part
-        self.buf1, self.tmp, self.buf2 = bufs
-        self.send1, self.recv1, self.send2, self.recv2 = sems
-        self.started = []
-
-    def go(self, copy):
-        copy.start()
-        self.started.append(copy)
-
-    def push(self):
-        at = self.at
-        for r in list(range(1, at.n)) + [0]:
-            there = at.slot(at.to(r, at.sib))
-            self.go(remote(self.part.at[there], self.buf1.at[r], self.send1.at[r], self.recv1.at[r], at.sibling()))
-
-    def arrived(self, r):
-        at = self.at
-        remote(self.buf1.at[r], self.buf1.at[r], self.send1.at[r], self.recv1.at[r], at.sibling()).wait_recv()
-        mine = self.part[at.slot(at.to(r))].astype(jnp.float32)
-        return mine + self.buf1[r].astype(jnp.float32)
-
-    def forward(self):
-        at = self.at
-        for r in range(1, at.n):
-            self.tmp[r] = self.arrived(r).astype(jnp.bfloat16)
-            self.go(remote(self.tmp.at[r], self.buf2.at[r], self.send2.at[r], self.recv2.at[r], (at.hi,) + at.to(r)))
-
-    def finish(self):
-        at = self.at
-        total = self.arrived(0)
-        for r in range(1, at.n):
-            remote(self.buf2.at[r], self.buf2.at[r], self.send2.at[r], self.recv2.at[r], (at.hi,) + at.to(r)).wait_recv()
-            total = total + self.buf2[r].astype(jnp.float32)
-        return total
 
     def drain(self):
         for copy in self.started:
             copy.wait_send()
+
+
+class CubeGather(Unit):
+    def __init__(self, at, turn, own, aim, sems):
+        super().__init__(at, turn, sems)
+        self.own, self.aim = own, aim
+
+    def push(self):
+        at = self.at
+        mine = self.aim(at.slot(0))
+        for r in (self.first, self.second):
+            self.go(self.own, mine, self.send1.at[r], self.recv1.at[r], at.device(r))
+        self.go(self.own, mine, self.send2.at[0], self.recv2.at[0], at.sibling())
+
+    def arrive(self, r, by):
+        at = self.at
+        here = self.aim(at.slot(r))
+        remote(here, here, self.send1.at[r], self.recv1.at[r], at.device(by)).wait_recv()
+        if r == self.first:
+            self.go(here, here, self.send1.at[3], self.recv1.at[3], at.device(self.second))
+        self.go(here, here, self.send2.at[r], self.recv2.at[r], at.sibling())
+
+    def forward(self):
+        self.arrive(self.first, self.first)
+        self.arrive(self.second, self.second)
+
+    def corner(self):
+        self.arrive(3, self.second)
+
+    def finish(self):
+        at = self.at
+        for r in range(N):
+            here = self.aim(at.slot(r, at.sib))
+            remote(here, here, self.send2.at[r], self.recv2.at[r], at.sibling()).wait_recv()
+        self.drain()
+
+
+class CubeScatter(Unit):
+    def __init__(self, at, turn, part, bufs, sems):
+        super().__init__(at, turn, sems)
+        self.part = part
+        self.buf1, self.tmp, self.buf2 = bufs
+
+    def push(self):
+        at = self.at
+        for r in (3, self.first, self.second, 0):
+            there = self.part(at.slot(r, at.sib))
+            self.go(there, self.buf1.at[r], self.send1.at[r], self.recv1.at[r], at.sibling())
+
+    def arrived(self, r):
+        at, buf = self.at, self.buf1.at[r]
+        remote(buf, buf, self.send1.at[r], self.recv1.at[r], at.sibling()).wait_recv()
+        return self.part(at.slot(r))[...].astype(jnp.float32) + buf[...].astype(jnp.float32)
+
+    def landed(self, r, by):
+        buf = self.buf2.at[r]
+        remote(buf, buf, self.send2.at[r], self.recv2.at[r], self.at.device(by)).wait_recv()
+        return buf[...].astype(jnp.float32)
+
+    def send(self, r, value, to):
+        self.tmp[r] = value.astype(jnp.bfloat16)
+        self.go(self.tmp.at[r], self.buf2.at[r], self.send2.at[r], self.recv2.at[r], self.at.device(to))
+
+    def forward(self):
+        self.send(3, self.arrived(3), self.first)
+        self.send(self.first, self.arrived(self.first), self.first)
+
+    def corner(self):
+        value = self.arrived(self.second)
+        self.send(self.second, value + self.landed(3, self.first), self.second)
+
+    def finish(self):
+        total = self.arrived(0)
+        for r in (self.first, self.second):
+            total = total + self.landed(r, r)
+        return total
+
+
+def row_units(rows):
+    half = rows // 2
+    return [pl.ds(u * half, half) for u in range(2)]
+
+
+def row_gathers(at, own, out, sems):
+    return [
+        CubeGather(at, u, own.at[span], lambda slot, span=span: out.at[slot, span], [s.at[u] for s in sems])
+        for u, span in enumerate(row_units(own.shape[0]))
+    ]
+
+
+def row_scatters(at, part, bufs, sems):
+    return [
+        CubeScatter(
+            at, u, lambda slot, span=span: part.at[slot, span],
+            [b.at[u] for b in bufs], [s.at[u] for s in sems],
+        )
+        for u, span in enumerate(row_units(part.shape[1]))
+    ]
 
 
 def params_kernel(far, ctx, shard, pad, *refs):
@@ -195,9 +234,10 @@
     at = Place(ctx)
     beyond = [(lax.rem(at.hi + h, far), at.lo, at.c) for h in range(1, far)]
     greet(at.cube() + beyond)
-    mine = at.slot((at.lo, at.c))
+    mine = at.slot(0)
     for h in range(1, far):
         remote(attn_ref, held.at[mine, at.hi], send_z.at[h], recv_z.at[h], beyond[h - 1]).start()
+    cots = row_gathers(at, cot_ref, cots_ref, cot_sems)
     gathers = []
     for h in range(far):
         origin = lax.rem(at.hi + far - h, far)
@@ -205,18 +245,24 @@
         if h:
             remote(own, own, send_z.at[h], recv_z.at[h], beyond[h - 1]).wait_recv()
         gather = CubeGather(
-            at, own, held, [s.at[h] for s in piece_sems],
-            lambda out, slot, origin=origin: out.at[slot, origin],
+            at, h, own, lambda slot, origin=origin: held.at[slot, origin],
+            [s.at[h] for s in piece_sems],
         )
         gather.push()
         gathers.append(gather)
-    held[mine, at.hi] = attn_ref[...]
-    cots = CubeGather(at, cot_ref, cots_ref, cot_sems)
-    cots.push()
-    cots_ref[mine] = cot_ref[...]
+        if h == 0:
+            held[mine, at.hi] = attn_ref[...]
+            for cot in cots:
+                cot.push()
+            cots_ref[mine] = cot_ref[...]
     for gather in gathers:
         gather.forward()
-    cots.forward()
+    for gather in gathers:
+        gather.corner()
+    for cot in cots:
+        cot.forward()
+    for cot in cots:
+        cot.corner()
     for gather in gathers:
         gather.finish()
     for g in range(0, far * 2 * ctx):
@@ -230,7 +276,8 @@
         cols = pl.ds(D + j * LANES, LANES)
         qkv_ref[:, cols] = flat[pl.ds(D * W + j * D, D), :].astype(jnp.bfloat16)
     small_ref[...] = flat[pl.ds(MATRIX_ROWS, SMALL_ROWS), :]
-    cots.finish()
+    for cot in cots:
+        cot.finish()
     for h in range(1, far):
         remote(attn_ref, held.at[mine, at.hi], send_z.at[h], recv_z.at[h], beyond[h - 1]).wait_send()
 
@@ -238,21 +285,43 @@
 def rows_kernel(ctx, own_ref, out_ref, *sems):
     at = Place(ctx)
     greet(at.cube())
-    gather = CubeGather(at, own_ref, out_ref, sems)
-    gather.push()
-    out_ref[at.slot((at.lo, at.c))] = own_ref[...]
-    gather.forward()
-    gather.finish()
+    gathers = row_gathers(at, own_ref, out_ref, sems)
+    for gather in gathers:
+        gather.push()
+    out_ref[at.slot(0)] = own_ref[...]
+    for gather in gathers:
+        gather.forward()
+    for gather in gathers:
+        gather.corner()
+    for gather in gathers:
+        gather.finish()
 
 
 def sum_kernel(ctx, part_ref, out_ref, buf1, tmp, buf2, *sems):
     at = Place(ctx)
     greet(at.cube())
-    scatter = CubeScatter(at, part_ref, (buf1, tmp, buf2), sems)
-    scatter.push()
-    scatter.forward()
-    out_ref[...] = scatter.finish()
-    scatter.drain()
+    scatters = row_scatters(at, part_ref, (buf1, tmp, buf2), sems)
+    for scatter in scatters:
+        scatter.push()
+    for scatter in scatters:
+        scatter.forward()
+    for scatter in scatters:
+        scatter.corner()
+    for scatter, span in zip(scatters, row_units(out_ref.shape[0])):
+        out_ref[span, :] = scatter.finish()
+        scatter.drain()
+
+
+def stream_gather_kernel(ctx, own_ref, out_ref, send, recv):
+    hi, lo, c = lax.axis_index("hi"), lax.axis_index("lo"), lax.axis_index("ctx")
+    others = [lax.rem(c + d, ctx) for d in range(1, ctx)]
+    greet([(hi, lo, other) for other in others])
+    for d, other in enumerate(others):
+        remote(own_ref, out_ref.at[c], send.at[d], recv.at[d], (hi, lo, other)).start()
+    out_ref[c] = own_ref[...]
+    for d, other in enumerate(others):
+        here = out_ref.at[lax.rem(c + ctx - d - 1, ctx)]
+        remote(own_ref, here, send.at[d], recv.at[d], (hi, lo, other)).wait()
 
 
 def stream_sum_kernel(ctx, part_ref, out_ref, buf, send, recv):
@@ -273,15 +342,16 @@
 
 def grads_kernel(far, ctx, shard, pad, *refs):
     qkv_ref, gout_ref, small_ref, part_ref, attn_ref, sum_ref = refs[:6]
-    flat, held, col, low, buf3 = refs[6:11]
-    attn_bufs, sum_bufs = refs[11:14], refs[14:17]
-    send_z, recv_z = refs[17:19]
-    attn_sems, sum_sems = refs[19:23], refs[23:27]
+    flat, held, low, buf3 = refs[6:10]
+    attn_bufs, sum_bufs = refs[10:13], refs[13:16]
+    send_z, recv_z = refs[16:18]
+    attn_sems, sum_sems = refs[18:22], refs[22:26]
     at = Place(ctx)
     beyond = [(lax.rem(at.hi + h, far), at.lo, at.c) for h in range(1, far)]
     greet(at.cube() + beyond)
-    sums = CubeScatter(at, part_ref, sum_bufs, sum_sems)
-    sums.push()
+    sums = row_scatters(at, part_ref, sum_bufs, sum_sems)
+    for unit in sums:
+        unit.push()
     for j in range(W):
         cols = pl.ds(j * LANES, LANES)
         flat[pl.ds(j, D, stride=W), :] = qkv_ref[:, cols]
@@ -294,25 +364,38 @@
     for g in range(far * 2 * ctx):
         block = flat[pl.ds(g * shard, pad), :]
         held[g % (2 * ctx), g // (2 * ctx)] = block.astype(jnp.bfloat16)
-    grads = CubeScatter(at, held, attn_bufs, attn_sems)
-    grads.push()
-    grads.forward()
-    sums.forward()
-    col[...] = grads.finish()
-    low[...] = col[...].astype(jnp.bfloat16)
+    grads = []
+    for h in list(range(1, far)) + [0]:
+        origin = lax.rem(at.hi + h, far)
+        unit = CubeScatter(
+            at, h, lambda slot, origin=origin: held.at[slot, origin],
+            [b.at[h] for b in attn_bufs], [s.at[h] for s in attn_sems],
+        )
+        unit.push()
+        grads.append(unit)
+    for unit in grads:
+        unit.forward()
+    for unit in grads:
+        unit.corner()
+    for unit in sums:
+        unit.forward()
     crossing = []
     for h in range(1, far):
-        copy = remote(low.at[beyond[h - 1][0]], buf3.at[h], send_z.at[h], recv_z.at[h], beyond[h - 1])
+        low[h] = grads[h - 1].finish().astype(jnp.bfloat16)
+        copy = remote(low.at[h], buf3.at[h], send_z.at[h], recv_z.at[h], beyond[h - 1])
         copy.start()
         crossing.append(copy)
-    sum_ref[...] = sums.finish()
-    total = col[at.hi]
+    total = grads[far - 1].finish()
+    for unit in sums:
+        unit.corner()
+    for unit, span in zip(sums, row_units(sum_ref.shape[0])):
+        sum_ref[span, :] = unit.finish()
     for h in range(1, far):
         crossing[h - 1].wait()
         total = total + buf3[h].astype(jnp.float32)
     attn_ref[...] = total
-    grads.drain()
-    sums.drain()
+    for unit in grads + sums:
+        unit.drain()
 
 
 def call(kernel, outs, scratch, number, *args):
@@ -340,7 +423,7 @@
 def gather_params(attn_rows, cot_low, far, ctx):
     shard = attn_rows.shape[0]
     pad = padded(shard)
-    cube, n = 2 * ctx, ctx
+    cube = 2 * ctx
     total = shard * far * cube + pad - shard
     attn_rows = jnp.pad(attn_rows, ((0, pad - shard), (0, 0)))
     bf16 = jnp.bfloat16
@@ -356,20 +439,30 @@
         dma(far),
         dma(far),
     ]
-    scratch += [dma(far, n)] * 4 + [dma(n)] * 4
+    scratch += [dma(far, N)] * 4 + [dma(2, N)] * 4
     kernel = functools.partial(params_kernel, far, ctx, shard, pad)
     return call(kernel, outs, scratch, 0, attn_rows, cot_low)
 
 
 def gather_rows(rows_low, ctx):
     outs = [((2 * ctx,) + rows_low.shape, jnp.bfloat16)]
-    return call(functools.partial(rows_kernel, ctx), outs, [dma(ctx)] * 4, 1, rows_low)[0]
+    return call(functools.partial(rows_kernel, ctx), outs, [dma(2, N)] * 4, 1, rows_low)[0]
+
+
+def halves(block):
+    return pltpu.VMEM((2, N, block[0] // 2) + block[1:], jnp.bfloat16)
 
 
 def sum_rows(part, ctx):
     block = part.shape[1:]
-    scratch = [pltpu.VMEM((ctx,) + block, jnp.bfloat16)] * 3 + [dma(ctx)] * 4
+    scratch = [halves(block)] * 3 + [dma(2, N)] * 4
     return call(functools.partial(sum_kernel, ctx), [(block, jnp.float32)], scratch, 2, part)[0]
+
+
+def stream_gather(own, ctx):
+    scratch = [dma(ctx - 1), dma(ctx - 1)]
+    outs = [((ctx,) + own.shape, own.dtype)]
+    return call(functools.partial(stream_gather_kernel, ctx), outs, scratch, 5, own)[0]
 
 
 def stream_sum(part, ctx):
@@ -380,7 +473,7 @@
 
 def scatter_grads(grad_qkv, grad_out, small, part, shard, far, ctx):
     pad = padded(shard)
-    cube, n = 2 * ctx, ctx
+    cube = 2 * ctx
     total = shard * far * cube + pad - shard
     block = part.shape[1:]
     bf16 = jnp.bfloat16
@@ -388,12 +481,11 @@
     scratch = [
         pltpu.VMEM((total, LANES), jnp.float32),
         pltpu.VMEM((cube,) + column, bf16),
-        pltpu.VMEM(column, jnp.float32),
         pltpu.VMEM(column, bf16),
         pltpu.VMEM(column, bf16),
     ]
-    scratch += [pltpu.VMEM((n,) + column, bf16)] * 3 + [pltpu.VMEM((n,) + block, bf16)] * 3
-    scratch += [dma(far)] * 2 + [dma(n)] * 8
+    scratch += [pltpu.VMEM((far, N, pad, LANES), bf16)] * 3 + [halves(block)] * 3
+    scratch += [dma(far)] * 2 + [dma(far, N)] * 4 + [dma(2, N)] * 4
     kernel = functools.partial(grads_kernel, far, ctx, shard, pad)
     outs = [((pad, LANES), jnp.float32), (block, jnp.float32)]
     attn, out_sum = call(kernel, outs, scratch, 4, grad_qkv, grad_out, small, part)
@@ -441,10 +533,8 @@
     query_low = rotate(query_pre.reshape(rows, HEADS, HEAD), cos_heads, sin_heads).astype(bf16)
     key_low = rotate(key_pre.reshape(rows, KV_HEADS, HEAD), cos_heads, sin_heads).astype(bf16)
     kv_low = jnp.concatenate([key_low.reshape(rows, kv_width), value_pre.astype(bf16)], axis=1)
-    kv_all = lax.all_gather(
-        kv_low.reshape(micro_count, rows_own, 2 * kv_width), "ctx", axis=1, tiled=True
-    )
-    kv_all = kv_all.reshape(micro_count, stream, 2, KV_HEADS, HEAD)
+    kv_all = stream_gather(kv_low, ctx).reshape(ctx, micro_count, rows_own, 2 * kv_width)
+    kv_all = kv_all.transpose(1, 0, 2, 3).reshape(micro_count, stream, 2, KV_HEADS, HEAD)
     keys_all, values_all = kv_all[:, :, 0], kv_all[:, :, 1]
     query_low = query_low.reshape(micro_count, rows_own, KV_HEADS, groups, HEAD)
     scores = (

time: 221 us -> 211 us (0.955)
  Pallas kernels: 119 us -> 111 us
  blocking collectives: 6.02 us -> 0 us
  local copies, waits for them, and re-layouts: 24.4 us -> 27.4 us
    pallas_call x5 -> x6, Pallas kernels: 119 us -> 111 us  [call(): pl.pallas_call(kernel, out_shape=[jax.ShapeDtypeStruct(shape, kind) for s...]
    all_gather x1 -> x0, blocking collectives: 6.02 us -> none  [per_device(): lax.all_gather(kv_low.reshape(micro_count, rows_own, 2 * kv_width), 'ctx'...]
    unnamed x80 -> x82, local copies, waits for them, and re-layouts: 8.87 us -> 11.3 us
  transfers between devices with their start and end apart: 2 -> 2, of which waited for: 0 -> 0; matrix products, arithmetic and copies ran while one was open for 23% -> 25% of each run, Pallas kernels for 54% -> 53%
where the time goes in v3:
time: 211 us; the launch traced here: 210 us
  Pallas kernels  111 us (53%)
  matrix products  38.4 us (18%)
  local copies, waits for them, and re-layouts  27.4 us (13%)
  other arithmetic  17.8 us (8%)
  between operations  15 us (7%)
    pallas_call x6, Pallas kernels, call(): pl.pallas_call(kernel, out_shape=[jax.ShapeDtypeStruct(shape, kind) for s...  111 us
    unnamed x82, local copies, waits for them, and re-layouts  11.3 us
  transfers between devices with their start and end apart: 2, of which 0 were waited for; matrix products, arithmetic and copies ran while one was open for 25% of the time, Pallas kernels for 53%

profile of v3, /device:TPU:0, one launch (start us, length us, event | category | flops | bytes accessed | tf_op | source)
XLA Modules:
  0.0 210.2 jit_solution(5739066363699798862)
XLA Ops:
  11.6 35.1 %shard_map.84 = (bf16[896,1152]{1,0:T(8,128)(2,1)S(1)}, bf16[896,896]{1,0:T(8,128)(2,1)S(1)}, f32[24,128]{1,0:T(8,128)S(1)}, bf16[8,128,896]{2,1,0:T(8,128)(2,1)S(1)}) custom-call(bf16[464,128]{1,0:T(8,128)(2,1)S(1)} %pad.4.refs_0_, bf16[128,896]{1,0:T(8,128)(2,1)S(1)} %bitcast.206), custom_call_target="tpu_custom_call" | custom-call | tf_op jit(solution)/shard_map/pallas_call | solution.py:403
  51.5 2.2 %convolution_add_fusion = f32[128,1152]{1,0:T(8,128)S(1)} fusion(bf16[128,896]{1,0:T(8,128)(2,1)S(1)} %fusion.25, bf16[896,1152]{1,0:T(8,128)(2,1)} %copy-done, f32[1152]{0:T(1024)S(1)} %slice_bitcast_fusion.1), kind=kOutput, calls=%fused_computation.3 | convolution fusion | flops 264388608 | bytes 2888192 | tf_op jit(solution)/shard_map/dot_general | solution.py:531
  57.0 5.0 %shard_map.85 = bf16[4,128,256]{2,1,0:T(8,128)(2,1)S(1)} custom-call(bf16[128,256]{1,0:T(8,128)(2,1)S(1)} %pad_maximum_fusion.3.own_ref), custom_call_target="tpu_custom_call" | custom-call | tf_op jit(solution)/shard_map/pallas_call | solution.py:403
  67.2 2.0 concatenate.58
  72.7 2.6 %fusion.14 = bf16[2,64,2,7,64]{1,0,4,3,2:T(2,128)(2,1)} fusion(f32[2,64,2,7,32]{1,0,4,3,2:T(2,128)} %concatenate.58, f32[2,64,2,7,32]{1,0,4,3,2:T(2,128)S(1)} %concatenate.57, f32[2,64,2,7,64]{1,0,4,3,2:T(2,128)S(1)} %reshape.306, f32[2,64,64]{1,0,2:T(2,128)S(1)} %pad_maximum_fusion.5, f32[2,64,64]{1,0,2:T(2,128)S(1)} %pad_maximum_fusion.4), kind=kLoop, calls=%fused_computation.36 | loop fusion | flops 573440 | bytes 1212416 | tf_op jit(solution)/shard_map/convert_element_type | solution.py:533
  75.2 3.0 %fusion.63 = (f32[2,2,7,64]{3,2,1,0:T(8,128)S(1)}, f32[2,2,7,64,256]{4,3,2,1,0:T(8,128)}) fusion(pred[2,64,256]{2,1,0:T(8,128)(4,1)} %compare_and_fusion, bf16[2,64,2,7,64]{1,0,4,3,2:T(2,128)(2,1)} %fusion.14, bf16[2,256,1,2,64]{1,4,3,0,2:T(8,128)(2,1)S(1)} %copy-done.20), kind=kOutput, calls=%fused_computation.139 | convolution fusion | flops 60555520 | bytes 2235392 | tf_op jit(solution)/shard_map/sub | solution.py:545
  78.3 2.1 fusion.7
  82.5 14.3 %shard_map.86 = bf16[8,128,896]{2,1,0:T(8,128)(2,1)S(1)} custom-call(bf16[128,896]{1,0:T(8,128)(2,1)S(1)} %multiply_convert_fusion.3.own_ref), custom_call_target="tpu_custom_call" | custom-call | tf_op jit(solution)/shard_map/pallas_call | solution.py:403
  96.8 2.2 %fusion.59 = (bf16[1,4,152,896]{3,2,0,1:T(8,128)(2,1)S(1)}, bf16[1,4,152,896]{3,2,0,1:T(8,128)(2,1)S(1)}, bf16[1,4,152,896]{3,2,0,1:T(8,128)(2,1)S(1)}) fusion(bf16[3,4,152,896]{3,2,0,1:T(8,128)(2,1)} %bitcast.212), kind=kLoop, calls=%fused_computation.135 | loop fusion | bytes 6537216 | tf_op jit(solution)/shard_map/slice | solution.py:555
  99.0 1.5 fusion.69
  101.3 1.5 fusion.68
  102.8 2.6 %multiply_convert_fusion = (bf16[1024,608]{0,1:T(8,128)(2,1)S(1)}, bf16[1024,608]{0,1:T(8,128)(2,1)S(1)}, bf16[1024,608]{0,1:T(8,128)(2,1)S(1)}) fusion(f32[1024,608]{0,1:T(8,128)S(1)} %fusion.69, f32[1024,608]{0,1:T(8,128)S(1)} %fusion.68, bf16[1024,896]{1,0:T(8,128)(2,1)S(1)} %bitcast.200, bf16[608,896]{1,0:T(8,128)(2,1)S(1)} %bitcast.215), kind=kOutput, calls=%fused_computation.4 | convolution fusion | flops 1125023744 | bytes 11640832 | tf_op jit(solution)/shard_map/td,fd->tf/dot_general | solution.py:558
  105.4 1.5 convolution_convert_fusion.3
  106.9 3.6 %fusion.70 = f32[1024,896]{1,0:T(8,128)} fusion(bf16[1024,608]{0,1:T(8,128)(2,1)S(1)} %get-tuple-element.21, bf16[608,896]{1,0:T(8,128)(2,1)S(1)} %bitcast.218), kind=kOutput, calls=%fused_computation.142 | convolution fusion | flops 1115684864 | bytes 6004736 | tf_op jit(solution)/shard_map/tf,fd->td/dot_general | solution.py:564
  113.4 2.1 %pad_maximum_fusion = bf16[3,4,152,896]{3,2,0,1:T(8,128)(2,1)} fusion(bf16[1,4,152,896]{3,2,0,1:T(8,128)(2,1)S(1)} %bitcast.221, bf16[1,4,152,896]{3,2,0,1:T(8,128)(2,1)S(1)} %bitcast.220, bf16[1,4,152,896]{3,2,0,1:T(8,128)(2,1)S(1)} %bitcast.219), kind=kLoop, calls=%fused_computation.2 | loop fusion | flops 3268608 | bytes 6537216 | tf_op jit(solution)/shard_map/stack | solution.py:571
  116.8 4.2 %add_convert_fusion = bf16[1024,896]{1,0:T(8,128)(2,1)S(1)} fusion(f32[1024,896]{1,0:T(8,128)} %fusion.70, bf16[1024,608]{0,1:T(8,128)(2,1)} %copy-done.37, bf16[608,896]{1,0:T(8,128)(2,1)S(1)} %bitcast.216), kind=kOutput, calls=%fused_computation.1 | convolution fusion | flops 1117519872 | bytes 7839744 | tf_op jit(solution)/shard_map/tf,fd->td/dot_general | solution.py:565
  121.0 12.7 %shard_map.87 = f32[128,896]{1,0:T(8,128)S(1)} custom-call(bf16[8,128,896]{2,1,0:T(8,128)(2,1)S(1)} %bitcast.203), custom_call_target="tpu_custom_call" | custom-call | tf_op jit(solution)/shard_map/pallas_call | solution.py:403
  135.6 2.4 %fusion.2 = (f32[2,2,7,64]{3,2,1,0:T(8,128)S(1)}, f32[2,2,256,64,7]{2,3,4,1,0:T(8,128)S(1)}) fusion(f32[2,2,7,64,256]{4,3,2,1,0:T(8,128)} %get-tuple-element.43, f32[2,2,7,64]{3,2,1,0:T(8,128)S(1)} %copy-done.31, bf16[2,64,2,7,64]{1,4,3,2,0:T(8,128)(2,1)S(1)} %copy.87, bf16[2,256,1,2,64]{1,4,3,0,2:T(8,128)(2,1)S(1)} %copy-done.29), kind=kOutput, calls=%fused_computation.11 | convolution fusion | flops 60094720 | bytes 4044800 | tf_op jit(solution)/shard_map/mqkgd,mskd->mkgqs/dot_general | solution.py:581
  143.8 2.0 fusion.12
  146.2 5.0 %shard_map.88 = f32[128,256]{1,0:T(8,128)S(1)} custom-call(bf16[4,128,256]{2,1,0:T(8,128)(2,1)S(1)} %bitcast.205), custom_call_target="tpu_custom_call" | custom-call | tf_op jit(solution)/shard_map/pallas_call | solution.py:403
  155.2 2.7 %fusion.58.refs_0_ = f32[896,1152]{1,0:T(8,128)} fusion(bf16[128,896]{1,0:T(8,128)(2,1)S(1)} %copy-done.11, bf16[128,128]{0,1:T(8,128)(2,1)S(1)} %copy.94, bf16[128,128]{0,1:T(8,128)(2,1)S(1)} %copy.93, bf16[128,896]{0,1:T(8,128)(2,1)S(1)} %fusion.21), kind=kOutput, calls=%fused_computation.134 | convolution fusion | flops 265125888 | bytes 4653056 | tf_op jit(solution)/shard_map/td,te->de/dot_general | solution.py:613
  157.9 1.8 convolution_convert_fusion
  159.7 38.9 %shard_map.89 = (f32[464,128]{1,0:T(8,128)S(1)}, f32[128,896]{1,0:T(8,128)S(1)}) custom-call(f32[896,1152]{1,0:T(8,128)} %fusion.58.refs_0_, f32[896,896]{1,0:T(8,128)S(1)} %fusion.48.refs_1_, f32[24,128]{1,0:T(8,128)S(1)} %maximum_bitcast_fusion.1.refs_2_, bf16[8,128,896]{2,1,0:T(8,128)(2,1)S(1)} %bitcast.198), custom_call_target="tpu_custom_call" | custom-call | tf_op jit(solution)/shard_map/pallas_call | solution.py:403
  200.9 2.4 %convert.22 = f32[3,152,896]{2,1,0:T(8,128)} convert(bf16[3,152,896]{2,1,0:T(8,128)(2,1)} %bitcast.224) | non-fusion elementwise | flops 408576 | bytes 2451456 | tf_op jit(solution)/shard_map/convert_element_type | solution.py:574
  (184 shorter events, 42.0 us)
Async XLA Ops:
  7.2 44.2 %copy-start.8 = (bf16[2,64,896]{2,1,0:T(8,128)(2,1)S(1)}, bf16[2,64,896]{2,1,0:T(8,128)(2,1)}, u32[]{:S(2)}) copy-start(bf16[2,64,896]{2,1,0:T(8,128)(2,1)} %param.5) | copy-start | bytes 688132
  7.2 89.7 %all-gather.2.cloned.1.call-start = ((), (), s32[]{:S(2)}) async-start(), calls=%async_computation.1 | async-start | bytes 4085760 | tf_op jit(solution)/shard_map/all_gather | solution.py:509
  7.9 193.0 %reduce-scatter.4.cloned.1.call-start = ((), (), s32[]{:S(2)}) async-start(), calls=%async_computation.2 | async-start | bytes 4085760
  51.3 2.4 %copy-start.33 = (f32[128]{0:T(128)}, f32[128]{0:T(128)S(1)}, u32[]{:S(2)}) copy-start(f32[128]{0:T(128)S(1)} %rsqrt.20) | copy-start | bytes 1540
  51.5 3.0 %copy-start.10 = (bf16[128,896]{1,0:T(8,128)(2,1)}, bf16[128,896]{1,0:T(8,128)(2,1)S(1)}, u32[]{:S(2)}) copy-start(bf16[128,896]{1,0:T(8,128)(2,1)S(1)} %fusion.25) | copy-start | bytes 688132
  70.0 5.3 %copy-start.20 = (bf16[2,256,1,2,64]{1,4,3,0,2:T(8,128)(2,1)S(1)}, bf16[2,256,1,2,64]{1,4,3,0,2:T(8,128)(2,1)}, u32[]{:S(2)}) copy-start(bf16[2,256,1,2,64]{1,4,3,0,2:T(8,128)(2,1)} %copy.105) | copy-start | bytes 393220
  75.2 3.0 %copy-start.28 = (bf16[2,256,1,2,64]{1,4,3,0,2:T(8,128)(2,1)S(1)}, bf16[2,256,1,2,64]{1,4,3,0,2:T(8,128)(2,1)}, u32[]{:S(2)}) copy-start(bf16[2,256,1,2,64]{1,4,3,0,2:T(8,128)(2,1)} %copy.104) | copy-start | bytes 393220
  78.3 2.1 %copy-start.30 = (f32[2,2,7,64]{3,2,1,0:T(8,128)}, f32[2,2,7,64]{3,2,1,0:T(8,128)S(1)}, u32[]{:S(2)}) copy-start(f32[2,2,7,64]{3,2,1,0:T(8,128)S(1)} %get-tuple-element.42) | copy-start | bytes 21508
  99.0 3.8 %copy-start.18 = (bf16[1,4,152,896]{3,2,0,1:T(8,128)(2,1)}, bf16[1,4,152,896]{3,2,0,1:T(8,128)(2,1)S(1)}, u32[]{:S(2)}) copy-start(bf16[1,4,152,896]{3,2,0,1:T(8,128)(2,1)S(1)} %get-tuple-element.23) | copy-start | bytes 3268612
  99.0 2.3 %copy-start.5 = (bf16[8,128,896]{2,1,0:T(8,128)(2,1)S(1)}, bf16[8,128,896]{2,1,0:T(8,128)(2,1)}, u32[]{:S(2)}) copy-start(bf16[8,128,896]{2,1,0:T(8,128)(2,1)} %copy-done.4) | copy-start | bytes 5505028
  105.4 5.1 %copy-start.37 = (bf16[1024,608]{0,1:T(8,128)(2,1)}, bf16[1024,608]{0,1:T(8,128)(2,1)S(1)}, u32[]{:S(2)}) copy-start(bf16[1024,608]{0,1:T(8,128)(2,1)S(1)} %get-tuple-element.22) | copy-start | bytes 3735556
  105.4 6.5 %copy-start.38 = (bf16[1024,608]{0,1:T(8,128)(2,1)}, bf16[1024,608]{0,1:T(8,128)(2,1)S(1)}, u32[]{:S(2)}) copy-start(bf16[1024,608]{0,1:T(8,128)(2,1)S(1)} %get-tuple-element.20) | copy-start | bytes 3735556
  121.0 12.7 %copy-start.7 = (f32[128,896]{1,0:T(8,128)S(1)}, f32[128,896]{1,0:T(8,128)}, u32[]{:S(2)}) copy-start(f32[128,896]{1,0:T(8,128)} %copy-done.6) | copy-start | bytes 1376260
  121.0 12.9 %copy-start.3 = (bf16[2,64,896]{2,1,0:T(8,128)(2,1)S(1)}, bf16[2,64,896]{2,1,0:T(8,128)(2,1)}, u32[]{:S(2)}) copy-start(bf16[2,64,896]{2,1,0:T(8,128)(2,1)} %param.9) | copy-start | bytes 688132
  135.6 2.5 %copy-start.24 = (bf16[2,64,2,7,64]{1,4,3,2,0:T(8,128)(2,1)}, bf16[2,64,2,7,64]{1,4,3,2,0:T(8,128)(2,1)S(1)}, u32[]{:S(2)}) copy-start(bf16[2,64,2,7,64]{1,4,3,2,0:T(8,128)(2,1)S(1)} %copy.87) | copy-start | bytes 688132
  135.6 2.5 %copy-start.14 = (f32[2,2,7,64,256]{4,3,2,1,0:T(8,128)S(1)}, f32[2,2,7,64,256]{4,3,2,1,0:T(8,128)}, u32[]{:S(2)}) copy-start(f32[2,2,7,64,256]{4,3,2,1,0:T(8,128)} %get-tuple-element.43) | copy-start | bytes 5505028
  142.0 1.7 copy-start.25
  145.8 5.5 %copy-start.23 = (f32[128,64]{0,1:T(8,128)S(1)}, f32[128,64]{0,1:T(8,128)}, u32[]{:S(2)}) copy-start(f32[128,64]{0,1:T(8,128)} %copy-done.22) | copy-start | bytes 98308
  145.8 6.0 %copy-start.15 = (f32[128,14,64]{0,2,1:T(8,128)S(1)}, f32[128,14,64]{0,2,1:T(8,128)}, u32[]{:S(2)}) copy-start(f32[128,14,64]{0,2,1:T(8,128)} %reshape.314) | copy-start | bytes 1376260
  151.8 1.6 copy-start.1
  152.1 2.1 %copy-start.13 = (bf16[128,896]{0,1:T(8,128)(2,1)S(1)}, bf16[128,896]{0,1:T(8,128)(2,1)}, u32[]{:S(2)}) copy-start(bf16[128,896]{0,1:T(8,128)(2,1)} %copy-done.12) | copy-start | bytes 688132
  155.2 2.7 %copy-start.17 = (bf16[1,4,152,896]{3,2,0,1:T(8,128)(2,1)S(1)}, bf16[1,4,152,896]{3,2,0,1:T(8,128)(2,1)}, u32[]{:S(2)}) copy-start(bf16[1,4,152,896]{3,2,0,1:T(8,128)(2,1)} %copy-done.16) | copy-start | bytes 3268612
  155.2 2.7 %copy-start.39 = (bf16[1024,608]{0,1:T(8,128)(2,1)S(1)}, bf16[1024,608]{0,1:T(8,128)(2,1)}, u32[]{:S(2)}) copy-start(bf16[1024,608]{0,1:T(8,128)(2,1)} %copy-done.38) | copy-start | bytes 3735556
  159.7 38.9 %copy-start.36 = (f32[128]{0:T(128)S(1)}, f32[128]{0:T(128)}, u32[]{:S(2)}) copy-start(f32[128]{0:T(128)} %copy-done.35) | copy-start | bytes 1540
  (18 other events, 18.7 us)
Sparse Core Ops, SparseCore 0:
  9.6 71.4 all-gather.1
  115.7 66.2 reduce-scatter.3

commit v4 on v3

--- a/solution.py
+++ b/solution.py
@@ -22,12 +22,6 @@
     return (
         values * lax.rsqrt(jnp.mean(values * values, axis=-1, keepdims=True) + EPSILON) * gain_vec
     )
-
-
-def rotate(values, cosine, sine_table):
-    half_width = values.shape[-1] // 2
-    turned = jnp.concatenate([-values[..., half_width:], values[..., :half_width]], axis=-1)
-    return values * cosine + turned * sine_table
 
 
 def rotate_back(incoming, cosine, sine_table):
@@ -312,16 +306,36 @@
         scatter.drain()
 
 
-def stream_gather_kernel(ctx, own_ref, out_ref, send, recv):
+def queries_kernel(ctx, x_ref, gain_ref, w_ref, b_ref, cos_ref, sin_ref, *refs):
+    normed_ref, query_ref, kv_ref, own, send, recv = refs
     hi, lo, c = lax.axis_index("hi"), lax.axis_index("lo"), lax.axis_index("ctx")
     others = [lax.rem(c + d, ctx) for d in range(1, ctx)]
     greet([(hi, lo, other) for other in others])
+    x = x_ref[...].astype(jnp.float32)
+    normed = rms_norm(x, gain_ref[...]).astype(jnp.bfloat16)
+    normed_ref[...] = normed
+    cosine, sine = cos_ref[...], sin_ref[...]
+    lane = lax.broadcasted_iota(jnp.int32, cosine.shape, 1)
+    early = lax.rem(lane, HEAD) < HEAD // 2
+
+    def tile(pre):
+        ahead = pltpu.roll(pre, LANES - HEAD // 2, 1)
+        behind = pltpu.roll(pre, HEAD // 2, 1)
+        return pre * cosine + jnp.where(early, -ahead, behind) * sine
+
+    kv = jnp.dot(normed, w_ref[:, D:], preferred_element_type=jnp.float32) + b_ref[:, D:]
+    own[:, :LANES] = tile(kv[:, :LANES]).astype(jnp.bfloat16)
+    own[:, LANES:] = kv[:, LANES:].astype(jnp.bfloat16)
     for d, other in enumerate(others):
-        remote(own_ref, out_ref.at[c], send.at[d], recv.at[d], (hi, lo, other)).start()
-    out_ref[c] = own_ref[...]
+        remote(own, kv_ref.at[c], send.at[d], recv.at[d], (hi, lo, other)).start()
+    kv_ref[c] = own[...]
+    query = jnp.dot(normed, w_ref[:, :D], preferred_element_type=jnp.float32) + b_ref[:, :D]
+    for j in range(W):
+        span = slice(j * LANES, (j + 1) * LANES)
+        query_ref[:, span] = tile(query[:, span]).astype(jnp.bfloat16)
     for d, other in enumerate(others):
-        here = out_ref.at[lax.rem(c + ctx - d - 1, ctx)]
-        remote(own_ref, here, send.at[d], recv.at[d], (hi, lo, other)).wait()
+        here = kv_ref.at[lax.rem(c + ctx - d - 1, ctx)]
+        remote(own, here, send.at[d], recv.at[d], (hi, lo, other)).wait()
 
 
 def stream_sum_kernel(ctx, part_ref, out_ref, buf, send, recv):
@@ -459,10 +473,14 @@
     return call(functools.partial(sum_kernel, ctx), [(block, jnp.float32)], scratch, 2, part)[0]
 
 
-def stream_gather(own, ctx):
-    scratch = [dma(ctx - 1), dma(ctx - 1)]
-    outs = [((ctx,) + own.shape, own.dtype)]
-    return call(functools.partial(stream_gather_kernel, ctx), outs, scratch, 5, own)[0]
+def queries(x, gain, w_qkv, b_qkv, cosine, sine, ctx):
+    rows = x.shape[0]
+    kv = (rows, QKV - D)
+    bf16 = jnp.bfloat16
+    scratch = [pltpu.VMEM(kv, bf16), dma(ctx - 1), dma(ctx - 1)]
+    outs = [((rows, D), bf16), ((rows, D), bf16), ((ctx,) + kv, bf16)]
+    args = (x, gain[None], w_qkv, b_qkv[None], cosine, sine)
+    return call(functools.partial(queries_kernel, ctx), outs, scratch, 5, *args)
 
 
 def stream_sum(part, ctx):
@@ -526,14 +544,17 @@
     )
 
     x_float = tokens.reshape(rows, D).astype(f32)
-    normed, norm_pull = jax.vjp(rms_norm, x_float, gain_one)
-    normed_low = normed.astype(bf16)
-    qkv = jnp.dot(normed_low, w_qkv, preferred_element_type=f32) + b_qkv
-    query_pre, key_pre, value_pre = jnp.split(qkv, [D, D + kv_width], axis=1)
-    query_low = rotate(query_pre.reshape(rows, HEADS, HEAD), cos_heads, sin_heads).astype(bf16)
-    key_low = rotate(key_pre.reshape(rows, KV_HEADS, HEAD), cos_heads, sin_heads).astype(bf16)
-    kv_low = jnp.concatenate([key_low.reshape(rows, kv_width), value_pre.astype(bf16)], axis=1)
-    kv_all = stream_gather(kv_low, ctx).reshape(ctx, micro_count, rows_own, 2 * kv_width)
+    _, norm_pull = jax.vjp(rms_norm, x_float, gain_one)
+    normed_low, query_low, kv_all = queries(
+        tokens.reshape(rows, D),
+        gain_one,
+        w_qkv,
+        b_qkv,
+        jnp.concatenate([cosine, cosine], axis=-1),
+        jnp.concatenate([sine_table, sine_table], axis=-1),
+        ctx,
+    )
+    kv_all = kv_all.reshape(ctx, micro_count, rows_own, 2 * kv_width)
     kv_all = kv_all.transpose(1, 0, 2, 3).reshape(micro_count, stream, 2, KV_HEADS, HEAD)
     keys_all, values_all = kv_all[:, :, 0], kv_all[:, :, 1]
     query_low = query_low.reshape(micro_count, rows_own, KV_HEADS, groups, HEAD)
@@ -568,10 +589,13 @@
     grad_gate = jnp.einsum("tf,td->fd", gate_low, two_all, preferred_element_type=f32)
     grad_up = jnp.einsum("tf,td->fd", up_low, two_all, preferred_element_type=f32)
     grad_down = jnp.einsum("tf,td->fd", hidden_low, cot_all, preferred_element_type=f32)
-    ffn_part = jnp.stack([grad_gate.astype(bf16), grad_up.astype(bf16), grad_down.astype(bf16)])
-    ffn_part = ffn_part.reshape(3, far, units, D).transpose(1, 0, 2, 3).reshape(far, 3 * units, D)
-    ffn_grad = lax.psum_scatter(ffn_part, "hi", scatter_dimension=0, tiled=False)
-    ffn_grad = ffn_grad.astype(f32).reshape(3, units, D)
+    shares = [
+        lax.psum_scatter(
+            part.astype(bf16).reshape(far, units, D), "hi", scatter_dimension=0, tiled=False
+        )
+        for part in (grad_gate, grad_up, grad_down)
+    ]
+    ffn_grad = jnp.stack([share.astype(f32) for share in shares])
 
     d_second_part, d_gain_two = norm_two_pull(d_two)
     d_second = cot_low.astype(f32) + d_second_part

time: 211 us -> 234 us (1.11)
  waiting for transfers between devices: 0.72 us -> 26.2 us
  matrix products: 38.4 us -> 35 us
    unnamed x3 -> x7, waiting for transfers between devices: 0.7 us -> 26.2 us
    convert_element_type x4 -> x0, other arithmetic: 5.13 us -> none  [the longest x1 2.58 us: per_device(): rotate(query_pre.reshape(rows, HEADS, HEAD), cos_heads, sin_heads)]
    concatenate x2, local copies, waits for them, and re-layouts: 3.2 us -> 0.13 us  [the longest x1 0.06 us: rotary_tables(): sine_table = jnp.concatenate([jnp.sin(angles), jnp.sin(angles)], axis=-1)]
    dot_general x1, matrix products: 4.2 us -> 1.78 us  [per_device(): jnp.einsum('tf,fd->td', up_low, w_up, preferred_element_type=f32)]
    unnamed x82 -> x67, local copies, waits for them, and re-layouts: 11.3 us -> 10.4 us
  transfers between devices with their start and end apart: 2 -> 4, of which waited for: 0 -> 1; matrix products, arithmetic and copies ran while one was open for 25% -> 21% of each run, Pallas kernels for 53% -> 42%
where the time goes in v4:
time: 234 us; the launch traced here: 233 us
  Pallas kernels  111 us (47%)
  matrix products  35 us (15%)
  local copies, waits for them, and re-layouts  28.9 us (12%)
  waiting for transfers between devices  26.2 us (11%)
  other arithmetic  17.3 us (7%)
  between operations  14.5 us (6%)
    pallas_call x6, Pallas kernels, call(): pl.pallas_call(kernel, out_shape=[jax.ShapeDtypeStruct(shape, kind) for s...  111 us
    unnamed x7, waiting for transfers between devices  26.2 us
    unnamed x67, local copies, waits for them, and re-layouts  10.4 us
  transfers between devices with their start and end apart: 4, of which 1 were waited for; matrix products, arithmetic and copies ran while one was open for 21% of the time, Pallas kernels for 42%

profile of v4, /device:TPU:0, one launch (start us, length us, event | category | flops | bytes accessed | tf_op | source)
XLA Modules:
  0.0 233.3 jit_solution(12549098898530528709)
XLA Ops:
  9.8 33.6 %shard_map.84 = (bf16[896,1152]{1,0:T(8,128)(2,1)S(1)}, bf16[896,896]{1,0:T(8,128)(2,1)S(1)}, f32[24,128]{1,0:T(8,128)S(1)}, bf16[8,128,896]{2,1,0:T(8,128)(2,1)S(1)}) custom-call(bf16[464,128]{1,0:T(8,128)(2,1)S(1)} %pad.4.refs_0_, bf16[128,896]{1,0:T(8,128)(2,1)S(1)} %bitcast.184), custom_call_target="tpu_custom_call" | custom-call | tf_op jit(solution)/shard_map/pallas_call | solution.py:417
  50.6 5.4 %shard_map.85 = (bf16[128,896]{1,0:T(8,128)(2,1)S(1)}, bf16[128,896]{1,0:T(8,128)(2,1)S(1)}, bf16[4,128,256]{2,1,0:T(8,128)(2,1)S(1)}) custom-call(bf16[128,896]{1,0:T(8,128)(2,1)S(1)} %bitcast.175, f32[1,896]{1,0:T(1,128)S(1)} %bitcast.187, bf16[896,1152]{1,0:T(8,128)(2,1)S(1)} %copy-done.2, f32[1,1152]{1,0:T(1,128)S(1)} %bitcast.186, ...), custom_call_target="tpu_custom_call" | custom-call | tf_op jit(solution)/shard_map/pallas_call | solution.py:417
  57.3 1.7 copy.95
  60.2 2.0 fusion.52
  62.2 2.1 fusion.7
  65.7 14.3 %shard_map.86 = bf16[8,128,896]{2,1,0:T(8,128)(2,1)S(1)} custom-call(bf16[128,896]{1,0:T(8,128)(2,1)S(1)} %multiply_convert_fusion.3.own_ref), custom_call_target="tpu_custom_call" | custom-call | tf_op jit(solution)/shard_map/pallas_call | solution.py:417
  82.0 2.3 fusion.48
  87.7 3.4 %multiply_convert_fusion = (bf16[1024,608]{0,1:T(8,128)(2,1)}, bf16[1024,608]{0,1:T(8,128)(2,1)S(1)}, bf16[1024,608]{0,1:T(8,128)(2,1)S(1)}) fusion(f32[1024,608]{0,1:T(8,128)S(1)} %fusion.56, f32[1024,608]{0,1:T(8,128)S(1)} %fusion.55, bf16[1024,896]{1,0:T(8,128)(2,1)S(1)} %bitcast.179, bf16[608,896]{1,0:T(8,128)(2,1)S(1)} %bitcast.193), kind=kOutput, calls=%fused_computation.2 | convolution fusion | flops 1125023744 | bytes 11640832 | tf_op jit(solution)/shard_map/td,fd->tf/dot_general | solution.py:579
  91.1 2.0 fusion.57
  93.1 1.8 add_convert_fusion
  95.0 12.7 %shard_map.87 = f32[128,896]{1,0:T(8,128)S(1)} custom-call(bf16[8,128,896]{2,1,0:T(8,128)(2,1)S(1)} %bitcast.182), custom_call_target="tpu_custom_call" | custom-call | tf_op jit(solution)/shard_map/pallas_call | solution.py:417
  109.4 2.1 fusion.12
  111.6 1.7 fusion.2
  114.1 2.4 %convolution_convert_fusion.1 = bf16[608,896]{1,0:T(8,128)(2,1)} fusion(bf16[1024,608]{0,1:T(8,128)(2,1)S(1)} %copy-done.29, bf16[1024,896]{1,0:T(8,128)(2,1)S(1)} %bitcast.189), kind=kOutput, calls=%fused_computation.16 | convolution fusion | flops 1116229632 | bytes 4169728 | tf_op jit(solution)/shard_map/tf,td->fd/dot_general | solution.py:591
  116.6 2.4 %fusion.4 = bf16[2,2,7,64,256]{4,3,2,1,0:T(8,128)(2,1)S(1)} fusion(f32[2,2,256,64,7]{2,3,4,1,0:T(8,128)} %get-tuple-element.48, f32[2,2,7,64]{3,2,1,0:T(8,128)S(1)} %get-tuple-element.47, f32[2,2,7,64,256]{4,3,2,1,0:T(8,128)} %get-tuple-element.44, f32[2,2,7,64]{3,2,1,0:T(8,128)S(1)} %get-tuple-element.43), kind=kLoop, calls=%fused_computation.11 | loop fusion | flops 1835008 | bytes 4601856 | tf_op jit(solution)/shard_map/convert_element_type | solution.py:607
  120.1 5.0 %shard_map.88 = f32[128,256]{1,0:T(8,128)S(1)} custom-call(bf16[4,128,256]{2,1,0:T(8,128)(2,1)S(1)} %bitcast.183), custom_call_target="tpu_custom_call" | custom-call | tf_op jit(solution)/shard_map/pallas_call | solution.py:417
  130.2 2.7 %reshape.255 = f32[128,896]{0,1:T(8,128)} reshape(f32[2,64,2,7,64]{1,0,4,3,2:T(2,128)} %copy-done.13) | data formatting | bytes 917504 | tf_op jit(solution)/shard_map/reshape | solution.py:627
  141.9 2.5 %convolution_convert_fusion.2 = bf16[608,896]{1,0:T(8,128)(2,1)} fusion(bf16[1024,608]{0,1:T(8,128)(2,1)S(1)} %copy-done.26, bf16[1024,896]{1,0:T(8,128)(2,1)S(1)} %bitcast.180), kind=kOutput, calls=%fused_computation.17 | convolution fusion | flops 1116229632 | bytes 4169728 | tf_op jit(solution)/shard_map/tf,td->fd/dot_general | solution.py:590
  149.4 2.7 %fusion.47.refs_0_ = f32[896,1152]{1,0:T(8,128)} fusion(bf16[128,896]{1,0:T(8,128)(2,1)S(1)} %get-tuple-element.18, bf16[128,128]{0,1:T(8,128)(2,1)S(1)} %copy.88, bf16[128,128]{0,1:T(8,128)(2,1)S(1)} %copy.87, bf16[128,896]{0,1:T(8,128)(2,1)S(1)} %fusion.22), kind=kOutput, calls=%fused_computation.121 | convolution fusion | flops 265125888 | bytes 4653056 | tf_op jit(solution)/shard_map/td,te->de/dot_general | solution.py:637
  152.1 1.8 convolution_convert_fusion
  153.9 40.2 %shard_map.89 = (f32[464,128]{1,0:T(8,128)S(1)}, f32[128,896]{1,0:T(8,128)S(1)}) custom-call(f32[896,1152]{1,0:T(8,128)} %fusion.47.refs_0_, f32[896,896]{1,0:T(8,128)S(1)} %fusion.37.refs_1_, f32[24,128]{1,0:T(8,128)S(1)} %maximum_bitcast_fusion.1.refs_2_, bf16[8,128,896]{2,1,0:T(8,128)(2,1)S(1)} %bitcast.177), custom_call_target="tpu_custom_call" | custom-call | tf_op jit(solution)/shard_map/pallas_call | solution.py:417
  194.9 2.4 %convolution_convert_fusion.3 = bf16[608,896]{1,0:T(8,128)(2,1)} fusion(bf16[1024,608]{0,1:T(8,128)(2,1)S(1)} %copy-done.28, bf16[1024,896]{1,0:T(8,128)(2,1)S(1)} %bitcast.181), kind=kOutput, calls=%fused_computation.18 | convolution fusion | flops 1116229632 | bytes 4169728 | tf_op jit(solution)/shard_map/tf,td->fd/dot_general | solution.py:589
  198.9 25.4 %reduce-scatter.10.cloned.1.call-done = bf16[1,152,896]{2,1,0:T(8,128)(2,1)} async-done(((bf16[4,152,896]{2,1,0:T(8,128)(2,1)}), bf16[1,152,896]{2,1,0:T(8,128)(2,1)}) %reduce-scatter.10.cloned.1.call-update) | async-done | bytes 272400
  224.4 2.4 %maximum_convert_fusion = f32[3,152,896]{2,1,0:T(8,128)} fusion(bf16[1,152,896]{2,1,0:T(8,128)(2,1)} %reduce-scatter.14.cloned.1.call-done, bf16[1,152,896]{2,1,0:T(8,128)(2,1)} %reduce-scatter.12.cloned.1.call-done, bf16[1,152,896]{2,1,0:T(8,128)(2,1)} %reduce-scatter.10.cloned.1.call-done), kind=kLoop, calls=%fused_computation.36 | loop fusion | flops 1225728 | bytes 2451456 | tf_op jit(solution)/shard_map/stack | solution.py:598
  (159 shorter events, 43.9 us)
Async XLA Ops:
  7.2 41.8 %copy-start = (bf16[2,64,896]{2,1,0:T(8,128)(2,1)S(1)}, bf16[2,64,896]{2,1,0:T(8,128)(2,1)}, u32[]{:S(2)}) copy-start(bf16[2,64,896]{2,1,0:T(8,128)(2,1)} %param.5) | copy-start | bytes 688132
  7.2 74.8 %all-gather.2.cloned.1.call-start = ((), (), s32[]{:S(2)}) async-start(), calls=%async_computation.3 | async-start | bytes 4085760 | tf_op jit(solution)/shard_map/all_gather | solution.py:527
  7.9 191.0 %reduce-scatter.14.cloned.1.call-start = ((), (), s32[]{:S(2)}) async-start(), calls=%async_computation.6 | async-start | bytes 1361920
  59.9 2.4 %copy-start.17 = (bf16[2,64,2,7,64]{1,4,3,2,0:T(8,128)(2,1)}, bf16[2,64,2,7,64]{1,4,3,2,0:T(8,128)(2,1)S(1)}, u32[]{:S(2)}) copy-start(bf16[2,64,2,7,64]{1,4,3,2,0:T(8,128)(2,1)S(1)} %copy.77) | copy-start | bytes 688132
  60.0 4.3 %copy-start.21 = (bf16[2,256,1,2,64]{1,4,3,0,2:T(8,128)(2,1)}, bf16[2,256,1,2,64]{1,4,3,0,2:T(8,128)(2,1)S(1)}, u32[]{:S(2)}) copy-start(bf16[2,256,1,2,64]{1,4,3,0,2:T(8,128)(2,1)S(1)} %copy.96) | copy-start | bytes 393220
  60.0 2.2 copy-start.23
  65.0 15.0 %copy-start.14 = (bf16[128,896]{0,1:T(8,128)(2,1)}, bf16[128,896]{0,1:T(8,128)(2,1)S(1)}, u32[]{:S(2)}) copy-start(bf16[128,896]{0,1:T(8,128)(2,1)S(1)} %convert_element_type.103) | copy-start | bytes 688132
  82.0 2.5 %copy-start.5 = (bf16[8,128,896]{2,1,0:T(8,128)(2,1)S(1)}, bf16[8,128,896]{2,1,0:T(8,128)(2,1)}, u32[]{:S(2)}) copy-start(bf16[8,128,896]{2,1,0:T(8,128)(2,1)} %copy-done.4) | copy-start | bytes 5505028
  91.1 2.0 copy-start.27
  91.1 2.0 copy-start.25
  94.9 12.9 %copy-start.9 = (bf16[2,64,896]{2,1,0:T(8,128)(2,1)S(1)}, bf16[2,64,896]{2,1,0:T(8,128)(2,1)}, u32[]{:S(2)}) copy-start(bf16[2,64,896]{2,1,0:T(8,128)(2,1)} %param.9) | copy-start | bytes 688132
  109.4 2.2 copy-start.16
  109.4 2.2 copy-start.24
  111.6 2.5 %copy-start.29 = (bf16[1024,608]{0,1:T(8,128)(2,1)S(1)}, bf16[1024,608]{0,1:T(8,128)(2,1)}, u32[]{:S(2)}) copy-start(bf16[1024,608]{0,1:T(8,128)(2,1)} %get-tuple-element.26) | copy-start | bytes 3735556
  116.6 82.4 %reduce-scatter.12.cloned.1.call-start = ((), (), s32[]{:S(2)}) async-start(), calls=%async_computation.5 | async-start | bytes 1361920
  116.6 2.4 %copy-start.18 = (bf16[2,64,2,7,64]{1,4,3,2,0:T(8,128)(2,1)S(1)}, bf16[2,64,2,7,64]{1,4,3,2,0:T(8,128)(2,1)}, u32[]{:S(2)}) copy-start(bf16[2,64,2,7,64]{1,4,3,2,0:T(8,128)(2,1)} %copy-done.17) | copy-start | bytes 688132
  130.2 11.7 %copy-start.6 = (bf16[8,128,896]{2,1,0:T(8,128)(2,1)S(1)}, bf16[8,128,896]{2,1,0:T(8,128)(2,1)}, u32[]{:S(2)}) copy-start(bf16[8,128,896]{2,1,0:T(8,128)(2,1)} %copy-done.4) | copy-start | bytes 5505028
  144.4 2.8 %copy-start.3 = (bf16[896,1152]{1,0:T(8,128)(2,1)S(1)}, bf16[896,1152]{1,0:T(8,128)(2,1)}, u32[]{:S(2)}) copy-start(bf16[896,1152]{1,0:T(8,128)(2,1)} %copy-done.1) | copy-start | bytes 6193156
  144.4 80.0 %reduce-scatter.10.cloned.1.call-start = ((), (), s32[]{:S(2)}) async-start(), calls=%async_computation.4 | async-start | bytes 1361920
  149.4 2.7 %copy-start.20 = (bf16[1,4,152,896]{3,2,0,1:T(8,128)(2,1)S(1)}, bf16[1,4,152,896]{3,2,0,1:T(8,128)(2,1)}, u32[]{:S(2)}) copy-start(bf16[1,4,152,896]{3,2,0,1:T(8,128)(2,1)} %copy-done.19) | copy-start | bytes 3268612
  149.4 2.7 %copy-start.30 = (bf16[1024,608]{0,1:T(8,128)(2,1)S(1)}, bf16[1024,608]{0,1:T(8,128)(2,1)}, u32[]{:S(2)}) copy-start(bf16[1024,608]{0,1:T(8,128)(2,1)} %get-tuple-element.26) | copy-start | bytes 3735556
  153.9 41.0 %copy-start.7 = (bf16[8,128,896]{2,1,0:T(8,128)(2,1)S(1)}, bf16[8,128,896]{2,1,0:T(8,128)(2,1)}, u32[]{:S(2)}) copy-start(bf16[8,128,896]{2,1,0:T(8,128)(2,1)} %copy-done.4) | copy-start | bytes 5505028
  153.9 40.9 %copy-start.28 = (bf16[1024,608]{0,1:T(8,128)(2,1)S(1)}, bf16[1024,608]{0,1:T(8,128)(2,1)}, u32[]{:S(2)}) copy-start(bf16[1024,608]{0,1:T(8,128)(2,1)} %copy-done.27) | copy-start | bytes 3735556
  194.9 2.5 %copy-start.22 = (f32[128,896]{1,0:T(8,128)S(1)}, f32[128,896]{1,0:T(8,128)}, u32[]{:S(2)}) copy-start(f32[128,896]{1,0:T(8,128)} %get-tuple-element.49) | copy-start | bytes 1376260
  (11 other events, 16.3 us)
Sparse Core Ops, SparseCore 0:
  9.6 69.7 all-gather.1
  116.7 33.0 reduce-scatter.13
  152.1 26.9 reduce-scatter.11
  197.5 26.8 reduce-scatter.9

commit v5 on v4

--- a/solution.py
+++ b/solution.py
@@ -589,13 +589,10 @@
     grad_gate = jnp.einsum("tf,td->fd", gate_low, two_all, preferred_element_type=f32)
     grad_up = jnp.einsum("tf,td->fd", up_low, two_all, preferred_element_type=f32)
     grad_down = jnp.einsum("tf,td->fd", hidden_low, cot_all, preferred_element_type=f32)
-    shares = [
-        lax.psum_scatter(
-            part.astype(bf16).reshape(far, units, D), "hi", scatter_dimension=0, tiled=False
-        )
-        for part in (grad_gate, grad_up, grad_down)
-    ]
-    ffn_grad = jnp.stack([share.astype(f32) for share in shares])
+    ffn_part = jnp.stack([grad_gate.astype(bf16), grad_up.astype(bf16), grad_down.astype(bf16)])
+    ffn_part = ffn_part.reshape(3, far, units, D).transpose(1, 0, 2, 3).reshape(far, 3 * units, D)
+    ffn_grad = lax.psum_scatter(ffn_part, "hi", scatter_dimension=0, tiled=False)
+    ffn_grad = ffn_grad.astype(f32).reshape(3, units, D)
 
     d_second_part, d_gain_two = norm_two_pull(d_two)
     d_second = cot_low.astype(f32) + d_second_part

time: 234 us -> 208 us (0.89)
  waiting for transfers between devices: 26.2 us -> 4.5 us
  local copies, waits for them, and re-layouts: 28.9 us -> 21.5 us
  Pallas kernels: 111 us -> 117 us
  other arithmetic: 17.3 us -> 13.5 us
    unnamed x7 -> x3, waiting for transfers between devices: 26.2 us -> 4.5 us
    pallas_call x6, Pallas kernels: 111 us -> 117 us  [call(): pl.pallas_call(kernel, out_shape=[jax.ShapeDtypeStruct(shape, kind) for s...]
    convert_element_type x0 -> x1, other arithmetic: none -> 2.41 us  [per_device(): ffn_grad = ffn_grad.astype(f32).reshape(3, units, D)]
    unnamed x67 -> x63, local copies, waits for them, and re-layouts: 10.4 us -> 9.62 us
  transfers between devices with their start and end apart: 4 -> 2, of which waited for: 1 -> 1; matrix products, arithmetic and copies ran while one was open for 21% -> 15% of each run, Pallas kernels for 42% -> 51%
where the time goes in v5:
time: 208 us; the launch traced here: 205 us
  Pallas kernels  117 us (56%)
  matrix products  33.8 us (16%)
  local copies, waits for them, and re-layouts  21.5 us (10%)
  between operations  14.8 us (7%)
  other arithmetic  13.5 us (6%)
  waiting for transfers between devices  4.5 us (2%)
    pallas_call x6, Pallas kernels, call(): pl.pallas_call(kernel, out_shape=[jax.ShapeDtypeStruct(shape, kind) for s...  117 us
    unnamed x63, local copies, waits for them, and re-layouts  9.62 us
    unnamed x3, waiting for transfers between devices  4.5 us
  transfers between devices with their start and end apart: 2, of which 1 were waited for; matrix products, arithmetic and copies ran while one was open for 15% of the time, Pallas kernels for 51%

profile of v5, /device:TPU:0, one launch (start us, length us, event | category | flops | bytes accessed | tf_op | source)
XLA Modules:
  0.0 205.5 jit_solution(16961251725326424472)
XLA Ops:
  9.8 33.6 %shard_map.84 = (bf16[896,1152]{1,0:T(8,128)(2,1)S(1)}, bf16[896,896]{1,0:T(8,128)(2,1)S(1)}, f32[24,128]{1,0:T(8,128)S(1)}, bf16[8,128,896]{2,1,0:T(8,128)(2,1)S(1)}) custom-call(bf16[464,128]{1,0:T(8,128)(2,1)S(1)} %pad.4.refs_0_, bf16[128,896]{1,0:T(8,128)(2,1)S(1)} %bitcast.195), custom_call_target="tpu_custom_call" | custom-call | tf_op jit(solution)/shard_map/pallas_call | solution.py:417
  49.5 1.6 copy-done.2
  51.0 5.4 %shard_map.85 = (bf16[128,896]{1,0:T(8,128)(2,1)S(1)}, bf16[128,896]{1,0:T(8,128)(2,1)S(1)}, bf16[4,128,256]{2,1,0:T(8,128)(2,1)S(1)}) custom-call(bf16[128,896]{1,0:T(8,128)(2,1)S(1)} %bitcast.186, f32[1,896]{1,0:T(1,128)S(1)} %bitcast.198, bf16[896,1152]{1,0:T(8,128)(2,1)S(1)} %copy-done.2, f32[1,1152]{1,0:T(1,128)S(1)} %bitcast.197, ...), custom_call_target="tpu_custom_call" | custom-call | tf_op jit(solution)/shard_map/pallas_call | solution.py:417
  59.0 1.9 fusion.52
  61.0 2.1 %fusion.7 = bf16[2,64,2,7,64]{1,4,3,2,0:T(8,128)(2,1)S(1)} fusion(bf16[2,256,1,2,64]{1,4,3,0,2:T(8,128)(2,1)S(1)} %copy-done.24, f32[2,2,7,64,256]{4,3,2,1,0:T(8,128)} %get-tuple-element.44, f32[2,2,7,64]{3,2,1,0:T(8,128)S(1)} %get-tuple-element.43), kind=kOutput, calls=%fused_computation.24 | convolution fusion | flops 59752448 | bytes 2202624 | tf_op jit(solution)/shard_map/mkgqs,mskd->mqkgd/dot_general | solution.py:568
  64.5 14.3 %shard_map.86 = bf16[8,128,896]{2,1,0:T(8,128)(2,1)S(1)} custom-call(bf16[128,896]{1,0:T(8,128)(2,1)S(1)} %multiply_convert_fusion.3.own_ref), custom_call_target="tpu_custom_call" | custom-call | tf_op jit(solution)/shard_map/pallas_call | solution.py:417
  81.4 2.3 %fusion.48 = (bf16[1,4,152,896]{3,2,0,1:T(8,128)(2,1)S(1)}, bf16[1,4,152,896]{3,2,0,1:T(8,128)(2,1)S(1)}, bf16[1,4,152,896]{3,2,0,1:T(8,128)(2,1)S(1)}) fusion(bf16[3,4,152,896]{3,2,0,1:T(8,128)(2,1)} %bitcast.202), kind=kLoop, calls=%fused_computation.122 | loop fusion | bytes 6537216 | tf_op jit(solution)/shard_map/slice | solution.py:576
  85.6 1.5 fusion.55
  87.1 3.4 %multiply_convert_fusion = (bf16[1024,608]{0,1:T(8,128)(2,1)}, bf16[1024,608]{0,1:T(8,128)(2,1)S(1)}, bf16[1024,608]{0,1:T(8,128)(2,1)S(1)}) fusion(f32[1024,608]{0,1:T(8,128)S(1)} %fusion.56, f32[1024,608]{0,1:T(8,128)S(1)} %fusion.55, bf16[1024,896]{1,0:T(8,128)(2,1)S(1)} %bitcast.190, bf16[608,896]{1,0:T(8,128)(2,1)S(1)} %bitcast.207), kind=kOutput, calls=%fused_computation.3 | convolution fusion | flops 1125023744 | bytes 11640832 | tf_op jit(solution)/shard_map/td,fd->tf/dot_general | solution.py:579
  90.5 2.0 fusion.57
  92.5 2.5 %convolution_convert_fusion.3 = bf16[608,896]{1,0:T(8,128)(2,1)} fusion(bf16[1024,608]{0,1:T(8,128)(2,1)S(1)} %get-tuple-element.27, bf16[1024,896]{1,0:T(8,128)(2,1)S(1)} %bitcast.191), kind=kOutput, calls=%fused_computation.19 | convolution fusion | flops 1116229632 | bytes 4169728 | tf_op jit(solution)/shard_map/tf,td->fd/dot_general | solution.py:589
  95.0 2.5 %convolution_convert_fusion.2 = bf16[608,896]{1,0:T(8,128)(2,1)} fusion(bf16[1024,608]{0,1:T(8,128)(2,1)S(1)} %get-tuple-element.28, bf16[1024,896]{1,0:T(8,128)(2,1)S(1)} %bitcast.192), kind=kOutput, calls=%fused_computation.18 | convolution fusion | flops 1116229632 | bytes 4169728 | tf_op jit(solution)/shard_map/tf,td->fd/dot_general | solution.py:590
  97.4 1.8 add_convert_fusion
  99.2 12.7 %shard_map.87 = f32[128,896]{1,0:T(8,128)S(1)} custom-call(bf16[8,128,896]{2,1,0:T(8,128)(2,1)S(1)} %bitcast.193), custom_call_target="tpu_custom_call" | custom-call | tf_op jit(solution)/shard_map/pallas_call | solution.py:417
  113.7 3.4 %fusion.2 = (f32[2,2,7,64]{3,2,1,0:T(8,128)S(1)}, f32[2,2,256,64,7]{2,3,4,1,0:T(8,128)}) fusion(f32[2,2,7,64,256]{4,3,2,1,0:T(8,128)} %get-tuple-element.44, f32[2,2,7,64]{3,2,1,0:T(8,128)S(1)} %get-tuple-element.43, bf16[2,64,2,7,64]{1,4,3,2,0:T(8,128)(2,1)S(1)} %copy.85, bf16[2,256,1,2,64]{1,4,3,0,2:T(8,128)(2,1)} %copy.104), kind=kOutput, calls=%fused_computation.10 | convolution fusion | flops 60094720 | bytes 4044800 | tf_op jit(solution)/shard_map/mqkgd,mskd->mkgqs/dot_general | solution.py:602
  118.7 2.1 %pad_maximum_fusion = bf16[3,4,152,896]{3,2,0,1:T(8,128)(2,1)} fusion(bf16[1,4,152,896]{3,2,0,1:T(8,128)(2,1)S(1)} %bitcast.211, bf16[1,4,152,896]{3,2,0,1:T(8,128)(2,1)S(1)} %bitcast.206, bf16[1,4,152,896]{3,2,0,1:T(8,128)(2,1)S(1)} %bitcast.205), kind=kLoop, calls=%fused_computation.2 | loop fusion | flops 3268608 | bytes 6537216 | tf_op jit(solution)/shard_map/stack | solution.py:592
  120.9 2.0 fusion.12
  123.2 2.6 %fusion.4 = bf16[2,2,7,64,256]{4,3,2,1,0:T(8,128)(2,1)S(1)} fusion(f32[2,2,256,64,7]{2,3,4,1,0:T(8,128)} %get-tuple-element.48, f32[2,2,7,64]{3,2,1,0:T(8,128)S(1)} %get-tuple-element.47, f32[2,2,7,64,256]{4,3,2,1,0:T(8,128)} %get-tuple-element.44, f32[2,2,7,64]{3,2,1,0:T(8,128)S(1)} %get-tuple-element.43), kind=kLoop, calls=%fused_computation.12 | loop fusion | flops 1835008 | bytes 4601856 | tf_op jit(solution)/shard_map/convert_element_type | solution.py:604
  126.5 5.0 %shard_map.88 = f32[128,256]{1,0:T(8,128)S(1)} custom-call(bf16[4,128,256]{2,1,0:T(8,128)(2,1)S(1)} %bitcast.194), custom_call_target="tpu_custom_call" | custom-call | tf_op jit(solution)/shard_map/pallas_call | solution.py:417
  139.3 2.6 %fusion.47.refs_0_ = f32[896,1152]{1,0:T(8,128)} fusion(bf16[128,896]{1,0:T(8,128)(2,1)S(1)} %get-tuple-element.18, bf16[128,128]{0,1:T(8,128)(2,1)S(1)} %copy.94, bf16[128,128]{0,1:T(8,128)(2,1)S(1)} %copy.93, bf16[128,896]{0,1:T(8,128)(2,1)S(1)} %fusion.22), kind=kOutput, calls=%fused_computation.121 | convolution fusion | flops 265125888 | bytes 4653056 | tf_op jit(solution)/shard_map/td,te->de/dot_general | solution.py:634
  142.0 1.8 convolution_convert_fusion
  143.8 46.3 %shard_map.89 = (f32[464,128]{1,0:T(8,128)S(1)}, f32[128,896]{1,0:T(8,128)S(1)}) custom-call(f32[896,1152]{1,0:T(8,128)} %fusion.47.refs_0_, f32[896,896]{1,0:T(8,128)S(1)} %fusion.37.refs_1_, f32[24,128]{1,0:T(8,128)S(1)} %maximum_bitcast_fusion.1.refs_2_, bf16[8,128,896]{2,1,0:T(8,128)(2,1)S(1)} %bitcast.188), custom_call_target="tpu_custom_call" | custom-call | tf_op jit(solution)/shard_map/pallas_call | solution.py:417
  192.4 3.8 %reduce-scatter.4.cloned.1.call-done = bf16[1,456,896]{2,1,0:T(8,128)(2,1)} async-done(((bf16[4,456,896]{2,1,0:T(8,128)(2,1)}), bf16[1,456,896]{2,1,0:T(8,128)(2,1)}) %reduce-scatter.4.cloned.1.call-update) | async-done | bytes 817168
  196.2 2.4 %convert.17 = f32[3,152,896]{2,1,0:T(8,128)} convert(bf16[3,152,896]{2,1,0:T(8,128)(2,1)} %bitcast.214) | non-fusion elementwise | flops 408576 | bytes 2451456 | tf_op jit(solution)/shard_map/convert_element_type | solution.py:595
  (150 shorter events, 31.2 us)
Async XLA Ops:
  7.2 42.3 %copy-start = (bf16[2,64,896]{2,1,0:T(8,128)(2,1)S(1)}, bf16[2,64,896]{2,1,0:T(8,128)(2,1)}, u32[]{:S(2)}) copy-start(bf16[2,64,896]{2,1,0:T(8,128)(2,1)} %param.5) | copy-start | bytes 688132
  7.2 74.2 %all-gather.2.cloned.1.call-start = ((), (), s32[]{:S(2)}) async-start(), calls=%async_computation.1 | async-start | bytes 4085760 | tf_op jit(solution)/shard_map/all_gather | solution.py:527
  7.9 188.3 %reduce-scatter.4.cloned.1.call-start = ((), (), s32[]{:S(2)}) async-start(), calls=%async_computation.2 | async-start | bytes 4085760
  49.5 1.6 copy-start.2
  58.7 2.3 %copy-start.11 = (bf16[2,64,2,7,64]{1,4,3,2,0:T(8,128)(2,1)}, bf16[2,64,2,7,64]{1,4,3,2,0:T(8,128)(2,1)S(1)}, u32[]{:S(2)}) copy-start(bf16[2,64,2,7,64]{1,4,3,2,0:T(8,128)(2,1)S(1)} %copy.83) | copy-start | bytes 688132
  58.7 2.3 %copy-start.24 = (bf16[2,256,1,2,64]{1,4,3,0,2:T(8,128)(2,1)S(1)}, bf16[2,256,1,2,64]{1,4,3,0,2:T(8,128)(2,1)}, u32[]{:S(2)}) copy-start(bf16[2,256,1,2,64]{1,4,3,0,2:T(8,128)(2,1)} %copy.104) | copy-start | bytes 393220
  58.8 4.2 %copy-start.21 = (bf16[2,256,1,2,64]{1,4,3,0,2:T(8,128)(2,1)}, bf16[2,256,1,2,64]{1,4,3,0,2:T(8,128)(2,1)S(1)}, u32[]{:S(2)}) copy-start(bf16[2,256,1,2,64]{1,4,3,0,2:T(8,128)(2,1)S(1)} %copy.105) | copy-start | bytes 393220
  64.3 15.7 %copy-start.20 = (f32[128,32]{1,0:T(8,128)S(1)}, f32[128,32]{1,0:T(8,128)}, u32[]{:S(2)}) copy-start(f32[128,32]{1,0:T(8,128)} %copy-done.19) | copy-start | bytes 49156
  64.3 15.9 %copy-start.18 = (f32[128,32]{1,0:T(8,128)S(1)}, f32[128,32]{1,0:T(8,128)}, u32[]{:S(2)}) copy-start(f32[128,32]{1,0:T(8,128)} %copy-done.17) | copy-start | bytes 49156
  81.4 2.3 %copy-start.25 = (f32[128]{0:T(128)}, f32[128]{0:T(128)S(1)}, u32[]{:S(2)}) copy-start(f32[128]{0:T(128)S(1)} %add.90) | copy-start | bytes 1540
  81.4 2.5 %copy-start.5 = (bf16[8,128,896]{2,1,0:T(8,128)(2,1)S(1)}, bf16[8,128,896]{2,1,0:T(8,128)(2,1)}, u32[]{:S(2)}) copy-start(bf16[8,128,896]{2,1,0:T(8,128)(2,1)} %copy-done.4) | copy-start | bytes 5505028
  83.7 1.7 copy-start.13
  83.9 1.7 copy-start.9
  99.2 12.9 %copy-start.7 = (bf16[2,64,896]{2,1,0:T(8,128)(2,1)S(1)}, bf16[2,64,896]{2,1,0:T(8,128)(2,1)}, u32[]{:S(2)}) copy-start(bf16[2,64,896]{2,1,0:T(8,128)(2,1)} %param.9) | copy-start | bytes 688132
  113.7 3.4 %copy-start.10 = (bf16[8,128,896]{2,1,0:T(8,128)(2,1)S(1)}, bf16[8,128,896]{2,1,0:T(8,128)(2,1)}, u32[]{:S(2)}) copy-start(bf16[8,128,896]{2,1,0:T(8,128)(2,1)} %copy-done.8) | copy-start | bytes 5505028
  113.7 3.4 %copy-start.27 = (bf16[1024,608]{0,1:T(8,128)(2,1)S(1)}, bf16[1024,608]{0,1:T(8,128)(2,1)}, u32[]{:S(2)}) copy-start(bf16[1024,608]{0,1:T(8,128)(2,1)} %get-tuple-element.26) | copy-start | bytes 3735556
  117.2 1.6 copy-start.16
  123.2 2.6 %copy-start.12 = (bf16[2,64,2,7,64]{1,4,3,2,0:T(8,128)(2,1)S(1)}, bf16[2,64,2,7,64]{1,4,3,2,0:T(8,128)(2,1)}, u32[]{:S(2)}) copy-start(bf16[2,64,2,7,64]{1,4,3,2,0:T(8,128)(2,1)} %copy-done.11) | copy-start | bytes 688132
  125.8 5.8 %copy-start.22 = (bf16[2,256,1,2,64]{1,4,3,0,2:T(8,128)(2,1)S(1)}, bf16[2,256,1,2,64]{1,4,3,0,2:T(8,128)(2,1)}, u32[]{:S(2)}) copy-start(bf16[2,256,1,2,64]{1,4,3,0,2:T(8,128)(2,1)} %copy-done.21) | copy-start | bytes 393220
  132.8 2.2 %copy-start.23 = (f32[128,128]{1,0:T(8,128)S(1)}, f32[128,128]{1,0:T(8,128)}, u32[]{:S(2)}) copy-start(f32[128,128]{1,0:T(8,128)} %copy.89) | copy-start | bytes 196612
  136.2 1.6 copy-start.3
  139.3 2.7 %copy-start.14 = (bf16[1,4,152,896]{3,2,0,1:T(8,128)(2,1)S(1)}, bf16[1,4,152,896]{3,2,0,1:T(8,128)(2,1)}, u32[]{:S(2)}) copy-start(bf16[1,4,152,896]{3,2,0,1:T(8,128)(2,1)} %copy-done.13) | copy-start | bytes 3268612
  139.3 2.7 %copy-start.28 = (bf16[1024,608]{0,1:T(8,128)(2,1)S(1)}, bf16[1024,608]{0,1:T(8,128)(2,1)}, u32[]{:S(2)}) copy-start(bf16[1024,608]{0,1:T(8,128)(2,1)} %get-tuple-element.26) | copy-start | bytes 3735556
  143.8 46.3 %copy-start.26 = (f32[128]{0:T(128)S(1)}, f32[128]{0:T(128)}, u32[]{:S(2)}) copy-start(f32[128]{0:T(128)} %copy-done.25) | copy-start | bytes 1540
  (7 other events, 7.6 us)
Sparse Core Ops, SparseCore 0:
  9.6 69.7 all-gather.1
  121.0 75.1 reduce-scatter.3
